TPU v7x, 256 devices: a whole 4x4x8 slice. The times are simulated.
256 devices in a mesh: pole: 2 (over x_hi), fy: 8 (over z), fz: 16 (over y, x_lo, core).
Axes of the slice: x: 4 (x_hi: 2, x_lo: 2; x = x_hi * 2 + x_lo), y: 4, z: 8, core: 2. Of those that a mesh axis runs over, the one named last changes fastest.
Arguments:
- states: float32 [2, 128, 128, 256], P(None, 'fy', 'fz'), may hold values from -126 to 126
- potential: float32 [128, 128, 256], P('fy', 'fz'), may hold values from 0.5 to 3
Outputs:
- filtered: float32 [2, 128, 128, 256], P('pole', 'fy', 'fz')
- correlation_gram: float32 [2, 2], replicated
- energy_gram: float32 [2, 2], replicated
All inputs are finite; a program needn't handle non-finite values.
Results may differ from a plain program's by a relative error of at most 0.0003.
Values sent between devices are 32-bit elements; how exact they have to be, the bound alone decides.
A program may use at most 64 MiB of HBM per device.

v0:
```python
import math

import jax
import jax.numpy as jnp
from jax import lax
from jax.sharding import PartitionSpec as P

ITERS = 2


center_energy = 1.0
contour_radius = 1.0


def dft_table(length):
    indices = jnp.arange(length, dtype=jnp.int32)
    phases = (indices[:, None] * indices[None, :] % length).astype(jnp.float32) * (
        2.0 * math.pi / length
    )
    return (jnp.cos(phases), jnp.sin(phases))


def freq_squares(length, offset, extent):
    indices = offset + jnp.arange(extent, dtype=jnp.int32)
    signed = jnp.where(indices < length // 2, indices, indices - length).astype(jnp.float32) * (
        2.0 * math.pi / length
    )
    return signed * signed


def transform_axis(fields, matrices, pattern, orient, real_out):
    real_part, imag_part = fields
    cosine, sine_part = matrices

    def product(operand, matrix):
        return jnp.einsum(pattern, operand, matrix, precision=lax.Precision.HIGHEST)

    if imag_part is None:
        return (product(real_part, cosine), orient * product(real_part, sine_part))
    if real_out:
        return (product(real_part, cosine) - orient * product(imag_part, sine_part), None)
    return (
        product(real_part, cosine) - orient * product(imag_part, sine_part),
        product(imag_part, cosine) + orient * product(real_part, sine_part),
    )


def reshaped(fields, shape):
    return (fields[0].reshape(shape), fields[1].reshape(shape))


def across_y(fields):
    return (
        lax.all_to_all(fields[0], "fy", split_axis=1, concat_axis=2, tiled=True),
        lax.all_to_all(fields[1], "fy", split_axis=1, concat_axis=2, tiled=True),
    )


def across_z(fields):
    return (
        lax.all_to_all(fields[0], "fz", split_axis=1, concat_axis=2, tiled=True),
        lax.all_to_all(fields[1], "fz", split_axis=1, concat_axis=2, tiled=True),
    )


def forward(fields, tables):
    count_y = lax.axis_size("fy")
    count_z = lax.axis_size("fz")
    fields = transform_axis(fields, tables[0], "cyzx,xak->cayzk", -1.0, False)
    columns, blocks_x, cells_y, cells_z, local_kx = fields[0].shape
    merged = cells_z * local_kx
    fields = reshaped(fields, (columns, blocks_x, cells_y, merged))
    fields = across_y(fields)
    fields = reshaped(fields, (columns, count_y * cells_y, merged))
    fields = transform_axis(fields, tables[1], "cym,ybq->cbqm", -1.0, False)
    local_ky = fields[0].shape[2]
    fields = across_z(fields)
    fields = reshaped(fields, (columns, count_z, local_ky, cells_z, local_kx))
    return transform_axis(fields, tables[2], "ctqzk,tzw->cqkw", -1.0, False)


def backward(fields, tables, real_out):
    count_y = lax.axis_size("fy")
    count_z = lax.axis_size("fz")
    fields = transform_axis(fields, tables[3], "cqkw,wtz->ctqzk", 1.0, False)
    columns, blocks_z, local_ky, cells_z, local_kx = fields[0].shape
    merged = cells_z * local_kx
    fields = reshaped(fields, (columns, blocks_z, local_ky, merged))
    fields = across_z(fields)
    length_y = count_z * local_ky
    fields = reshaped(fields, (columns, length_y, merged))
    fields = transform_axis(fields, tables[4], "cym,yv->cvm", 1.0, False)
    cells_y = length_y // count_y
    fields = reshaped(fields, (columns, count_y, cells_y, merged))
    fields = across_y(fields)
    fields = reshaped(fields, (columns, count_y, cells_y, cells_z, local_kx))
    return transform_axis(fields, tables[5], "cayzk,akx->cyzx", 1.0, real_out)


def hamiltonian(fields, potential, tables):
    spectra = forward(fields, tables)
    kinetic = tables[6]
    applied = backward((spectra[0] * kinetic, spectra[1] * kinetic), tables, fields[1] is None)
    if fields[1] is None:
        return (applied[0] + potential * fields[0], None)
    return (applied[0] + potential * fields[0], applied[1] + potential * fields[1])


def build_tables(cells_y, cells_z, length_x):
    count_y = lax.axis_size("fy")
    count_z = lax.axis_size("fz")
    length_y = cells_y * count_y
    length_z = cells_z * count_z
    local_kx = length_x // count_y
    local_ky = length_y // count_z
    cos_x, sin_x = dft_table(length_x)
    cos_y, sin_y = dft_table(length_y)
    cos_z, sin_z = dft_table(length_z)
    x_forward = (
        cos_x.reshape(length_x, count_y, local_kx),
        sin_x.reshape(length_x, count_y, local_kx),
    )
    y_forward = (
        cos_y.reshape(length_y, count_z, local_ky),
        sin_y.reshape(length_y, count_z, local_ky),
    )
    z_forward = (
        cos_z.reshape(count_z, cells_z, length_z),
        sin_z.reshape(count_z, cells_z, length_z),
    )
    z_inverse = (
        cos_z.reshape(length_z, count_z, cells_z),
        sin_z.reshape(length_z, count_z, cells_z),
    )
    y_inverse = (cos_y, sin_y)
    x_inverse = (
        cos_x.reshape(count_y, local_kx, length_x),
        sin_x.reshape(count_y, local_kx, length_x),
    )
    grid_x = freq_squares(length_x, lax.axis_index("fy") * local_kx, local_kx)
    grid_y = freq_squares(length_y, lax.axis_index("fz") * local_ky, local_ky)
    grid_z = freq_squares(length_z, 0, length_z)
    kinetic = 0.5 * (grid_y[:, None, None] + grid_x[None, :, None] + grid_z[None, None, :])
    kinetic = kinetic / float(length_x * length_y * length_z)
    return (x_forward, y_forward, z_forward, z_inverse, y_inverse, x_inverse, kinetic)


def column_view(factor):
    return factor[:, None, None, None]


def scaled(fields, factor):
    factor_re = column_view(factor[0])
    factor_im = column_view(factor[1])
    if fields[1] is None:
        return (factor_re * fields[0], factor_im * fields[0])
    return (
        factor_re * fields[0] - factor_im * fields[1],
        factor_re * fields[1] + factor_im * fields[0],
    )


def added(first, second, orient):
    real_part = first[0] + orient * second[0]
    if first[1] is None:
        return (real_part, orient * second[1])
    if second[1] is None:
        return (real_part, first[1])
    return (real_part, first[1] + orient * second[1])


def bilinear(first, second):
    cell_axes = (1, 2, 3)
    real_part = jnp.sum(first[0] * second[0], axis=cell_axes)
    imag_part = jnp.zeros_like(real_part)
    if first[1] is not None and second[1] is not None:
        real_part = real_part - jnp.sum(first[1] * second[1], axis=cell_axes)
    if second[1] is not None:
        imag_part = jnp.sum(first[0] * second[1], axis=cell_axes)
    if first[1] is not None:
        imag_part = imag_part + jnp.sum(first[1] * second[0], axis=cell_axes)
    return (real_part, imag_part)


def quotient(upper, lower):
    denominator = lower[0] * lower[0] + lower[1] * lower[1]
    return (
        (upper[0] * lower[0] + upper[1] * lower[1]) / denominator,
        (upper[1] * lower[0] - upper[0] * lower[1]) / denominator,
    )


def summed(values):
    return lax.psum((values[0], values[1]), ("fy", "fz"))


def local(states, potential):
    columns = states.shape[0]
    cells_y = states.shape[1]
    cells_z = states.shape[2]
    length_x = states.shape[3]
    tables = build_tables(cells_y, cells_z, length_x)
    pole_count = lax.axis_size("pole")
    pole_angle = math.pi * (lax.axis_index("pole").astype(jnp.float32) + 0.5) / pole_count
    ones_column = jnp.ones((columns,), jnp.float32)
    shift_value = (
        (center_energy + contour_radius * jnp.cos(pole_angle)) * ones_column,
        contour_radius * jnp.sin(pole_angle) * ones_column,
    )
    weight_re = contour_radius * jnp.cos(pole_angle) / pole_count
    weight_im = contour_radius * jnp.sin(pole_angle) / pole_count
    solution = (jnp.zeros_like(states), jnp.zeros_like(states))
    residual = (states, None)
    direction = (states, None)
    res_norm = summed(bilinear(residual, residual))
    for iteration in range(ITERS):
        shifted_image = added(
            scaled(direction, shift_value), hamiltonian(direction, potential, tables), -1.0
        )
        step_size = quotient(res_norm, summed(bilinear(direction, shifted_image)))
        solution = added(solution, scaled(direction, step_size), 1.0)
        residual = added(residual, scaled(shifted_image, step_size), -1.0)
        if iteration + 1 < ITERS:
            next_norm = summed(bilinear(residual, residual))
            update_ratio = quotient(next_norm, res_norm)
            direction = added(residual, scaled(direction, update_ratio), 1.0)
            res_norm = next_norm
    contribution = weight_re * solution[0] - weight_im * solution[1]
    owned_cols = columns // pole_count
    filter_block = lax.psum(contribution, "pole")
    owned = lax.dynamic_slice_in_dim(
        filter_block, lax.axis_index("pole") * owned_cols, owned_cols, 0
    )
    whole_re, whole_im = forward((filter_block, None), tables)
    kinetic = tables[6]
    correlation_part = jnp.einsum(
        "iyzx,jyzx->ij", filter_block, filter_block, precision=lax.Precision.HIGHEST
    )
    energy_part = jnp.einsum(
        "iyzx,jyzx->ij", filter_block * potential, filter_block, precision=lax.Precision.HIGHEST
    )
    energy_part = energy_part + jnp.einsum(
        "iqkw,jqkw->ij", whole_re * kinetic, whole_re, precision=lax.Precision.HIGHEST
    )
    energy_part = energy_part + jnp.einsum(
        "iqkw,jqkw->ij", whole_im * kinetic, whole_im, precision=lax.Precision.HIGHEST
    )
    correlation_sum, energy_sum = lax.psum((correlation_part, energy_part), ("fy", "fz"))
    cell_count = float(length_x * cells_y * lax.axis_size("fy") * cells_z * lax.axis_size("fz"))
    return (owned, correlation_sum / cell_count, energy_sum / cell_count)


def solution(mesh):
    placed = (P(None, "fy", "fz", None), P("fy", "fz", None))
    return jax.shard_map(
        local,
        mesh=mesh,
        in_specs=placed,
        out_specs=(P("pole", "fy", "fz", None), P(), P()),
        check_vma=False,
    )
```

profile of v0, /device:TPU:1, one launch (start us, length us, event | category | flops | bytes accessed | tf_op | source)
XLA Modules:
  0.0 1496.3 jit_solution(541251558083436471)
XLA Ops:
  7.2 3.0 convolution_bitcast_fusion.1
  11.5 9.1 all-to-all-start
  24.2 6.9 all-to-all-done
  31.0 3.4 all-to-all-start.1
  35.3 8.5 all-to-all-done.1
  45.2 8.9 all-to-all-start.2
  56.3 5.1 all-to-all-done.2
  61.3 4.6 all-to-all-start.3
  70.1 3.0 all-to-all-done.3
  83.0 4.8 all-to-all-start.4
  90.3 4.6 all-to-all-done.4
  95.0 4.3 all-to-all-start.5
  100.0 6.6 all-to-all-done.5
  107.9 3.4 all-to-all-start.6
  113.4 8.1 all-to-all-done.6
  121.4 3.4 all-to-all-start.7
  125.4 8.7 all-to-all-done.7
  138.5 278.7 %all-reduce.3 = (f32[2]{0:T(128)S(1)}, f32[2]{0:T(128)S(1)}, f32[2]{0:T(128)S(1)}) all-reduce(f32[2]{0:T(128)S(1)} %get-tuple-element.12, f32[2]{0:T(128)S(1)} %get-tuple-element.11, f32[2]{0:T(128)S(1)} %get-tuple-element.10), channel_id=1, replica_groups=mesh['pole'=2,'fy'=8,'fz'=16] {'fy','fz'}, use_global_device_ids=true, to_apply=%region_1.2 | all-reduce | flops 6 | bytes 48 | tf_op jit(solution)/shard_map/psum | solution.py:194
  417.5 275.7 %all-reduce.2 = (f32[2]{0:T(128)S(1)}, f32[2]{0:T(128)S(1)}) all-reduce(f32[2]{0:T(128)S(1)} %add.572, f32[2]{0:T(128)S(1)} %sub.114), channel_id=1, replica_groups=mesh['pole'=2,'fy'=8,'fz'=16] {'fy','fz'}, use_global_device_ids=true, to_apply=%region_10.11 | all-reduce | flops 4 | bytes 32 | tf_op jit(solution)/shard_map/psum | solution.py:194
  699.5 5.6 all-to-all-start.9
  710.5 5.0 all-to-all-done.9
  715.5 3.4 all-to-all-start.8
  719.6 8.6 all-to-all-done.8
  729.7 6.8 all-to-all-start.11
  738.5 5.1 all-to-all-done.11
  743.7 4.8 all-to-all-start.10
  752.6 3.0 all-to-all-done.10
  765.6 4.6 all-to-all-start.12
  772.7 4.6 all-to-all-done.12
  777.3 4.3 all-to-all-start.13
  782.3 6.6 all-to-all-done.13
  790.3 3.4 all-to-all-start.14
  795.7 8.1 all-to-all-done.14
  803.8 3.4 all-to-all-start.15
  807.7 2.6 convolution_bitcast_fusion.2
  810.3 6.2 all-to-all-done.15
  822.9 278.6 %all-reduce.1 = (f32[2]{0:T(128)S(1)}, f32[2]{0:T(128)S(1)}) all-reduce(f32[2]{0:T(128)S(1)} %add.591, f32[2]{0:T(128)S(1)} %sub.127), channel_id=1, replica_groups=mesh['pole'=2,'fy'=8,'fz'=16] {'fy','fz'}, use_global_device_ids=true, to_apply=%region_16.17 | all-reduce | flops 4 | bytes 32 | tf_op jit(solution)/shard_map/psum | solution.py:194
  1103.8 33.5 %all-reduce.6.cloned.1.call-done = f32[2,16,8,256]{3,2,1,0:T(8,128)} async-done(((f32[2,16,8,256]{3,2,1,0:T(8,128)}), f32[2,16,8,256]{3,2,1,0:T(8,128)}) %all-reduce.6.cloned.1.call-update) | async-done | bytes 262160 | tf_op jit(solution)/shard_map/psum | solution.py:230
  1137.3 2.9 convolution_bitcast_fusion
  1141.6 7.1 all-to-all-start.16
  1154.6 4.1 all-to-all-done.16
  1158.7 3.4 all-to-all-start.17
  1162.9 8.6 all-to-all-done.17
  1172.9 8.1 all-to-all-start.18
  1183.2 5.1 all-to-all-done.18
  1188.2 4.6 all-to-all-start.19
  1197.0 3.0 all-to-all-done.19
  1212.6 275.9 %all-reduce = (f32[2,2]{1,0:T(2,128)S(1)}, f32[2,2]{1,0:T(2,128)S(1)}) all-reduce(f32[2,2]{1,0:T(2,128)S(1)} %convolution_bitcast_fusion.11, f32[2,2]{1,0:T(2,128)S(1)} %fusion.35), channel_id=1, replica_groups=mesh['pole'=2,'fy'=8,'fz'=16] {'fy','fz'}, use_global_device_ids=true, to_apply=%region_18.19 | all-reduce | flops 8 | bytes 64 | tf_op jit(solution)/shard_map/psum | solution.py:248
  (142 shorter events, 109.1 us)
Async XLA Ops:
  11.5 9.2 copy-start
  11.5 19.5 %all-to-all-start = ((f32[2,8,16,256]{3,2,0,1:T(8,128)}), f32[2,8,16,256]{3,2,0,1:T(8,128)S(1)}, u32[]{:S(2)}, u32[]{:S(2)}) async-start(f32[2,8,16,256]{3,2,0,1:T(8,128)} %reshape.729), calls=%async_computation | async-start | bytes 524288 | tf_op jit(solution)/shard_map/all_to_all | solution.py:54
  31.0 12.8 all-to-all-start.1
  45.2 16.1 %all-to-all-start.2 = ((f32[2,16,8,256]{3,2,0,1:T(8,128)}), f32[2,16,8,256]{3,2,0,1:T(8,128)S(1)}, u32[]{:S(2)}, u32[]{:S(2)}) async-start(f32[2,16,8,256]{3,2,0,1:T(8,128)} %fusion.21), calls=%async_computation.2 | async-start | bytes 524288 | tf_op jit(solution)/shard_map/all_to_all | solution.py:61
  61.3 11.7 all-to-all-start.3
  83.0 11.9 all-to-all-start.4
  95.0 11.6 all-to-all-start.5
  107.9 13.5 all-to-all-start.6
  121.4 12.7 all-to-all-start.7
  134.6 1.9 copy-start.2
  417.2 276.6 %copy-start.4 = (f32[2]{0:T(128)}, f32[2]{0:T(128)S(1)}, u32[]{:S(2)}) copy-start(f32[2]{0:T(128)S(1)} %get-tuple-element.39) | copy-start | bytes 28
  693.3 0.5 copy-start.6
  693.3 0.5 copy-start.8
  699.5 16.0 %all-to-all-start.9 = ((f32[2,8,16,256]{3,2,0,1:T(8,128)}), f32[2,8,16,256]{3,2,0,1:T(8,128)S(1)}, u32[]{:S(2)}, u32[]{:S(2)}) async-start(f32[2,8,16,256]{3,2,0,1:T(8,128)} %reshape.732), calls=%async_computation.9 | async-start | bytes 524288 | tf_op jit(solution)/shard_map/all_to_all | solution.py:55
  715.5 12.8 all-to-all-start.8
  729.7 14.0 all-to-all-start.11
  743.7 11.9 all-to-all-start.10
  765.6 11.7 all-to-all-start.12
  777.3 11.6 all-to-all-start.13
  790.3 13.6 all-to-all-start.14
  803.8 12.7 all-to-all-start.15
  807.2 330.0 %all-reduce.6.cloned.1.call-start = ((), (), s32[]{:S(2)}) async-start(), calls=%async_computation.20 | async-start | bytes 524288 | tf_op jit(solution)/shard_map/psum | solution.py:230
  817.0 1.9 copy-start.3
  818.9 1.9 copy-start.10
  1101.5 0.7 copy-start.7
  1101.5 0.7 copy-start.9
  1102.2 0.7 copy-start.5
  1141.6 7.1 copy-start.1
  1141.6 17.1 %all-to-all-start.16 = ((f32[2,8,16,256]{3,2,0,1:T(8,128)}), f32[2,8,16,256]{3,2,0,1:T(8,128)S(1)}, u32[]{:S(2)}, u32[]{:S(2)}) async-start(f32[2,8,16,256]{3,2,0,1:T(8,128)} %reshape.733), calls=%async_computation.16 | async-start | bytes 524288 | tf_op jit(solution)/shard_map/all_to_all | solution.py:54
  1158.7 12.7 all-to-all-start.17
  1172.9 15.3 %all-to-all-start.18 = ((f32[2,16,8,256]{3,2,0,1:T(8,128)}), f32[2,16,8,256]{3,2,0,1:T(8,128)S(1)}, u32[]{:S(2)}, u32[]{:S(2)}) async-start(f32[2,16,8,256]{3,2,0,1:T(8,128)} %fusion.13), calls=%async_computation.18 | async-start | bytes 524288 | tf_op jit(solution)/shard_map/all_to_all | solution.py:61
  1188.2 11.8 all-to-all-start.19
Sparse Core Ops, SparseCore 0:
  1103.9 33.2 all-reduce.5
where the time goes:
time: 1500 us
  blocking collectives  1110 us (74%)
  waiting for transfers between devices  153 us (10%)
  starting transfers between devices  102 us (7%)
  matrix products  93.8 us (6%)
  local copies, waits for them, and re-layouts  21.1 us (1%)
  between operations  15.3 us (1%)
    psum x3, blocking collectives, summed(): return lax.psum((values[0], values[1]), ('fy', 'fz'))  833 us
    psum x1, blocking collectives, local(): lax.psum((correlation_part, energy_part), ('fy', 'fz'))  276 us
    dot_general x54, matrix products, product(): return jnp.einsum(pattern, operand, matrix, precision=lax.Precision.HIGHEST)  83.7 us
    all_to_all x5, waiting for transfers between devices, across_y(): lax.all_to_all(fields[1], 'fy', split_axis=1, concat_axis=2, tiled=True)  37 us
    all_to_all x5, waiting for transfers between devices, across_y(): lax.all_to_all(fields[0], 'fy', split_axis=1, concat_axis=2, tiled=True)  35.8 us
    psum x1, waiting for transfers between devices, local(): filter_block = lax.psum(contribution, 'pole')  33.5 us
    all_to_all x5, starting transfers between devices, across_z(): lax.all_to_all(fields[0], 'fz', split_axis=1, concat_axis=2, tiled=True)  31.3 us
  transfers between devices with their start and end apart: 21, of which 21 were waited for; matrix products, arithmetic and copies ran while one was open for 3% of the time, Pallas kernels for 0%

commit v1 on v0

v1 whole, which is shorter than its diff:
```python
import functools
import math

import jax
import jax.numpy as jnp
import numpy as np
from jax import lax
from jax.experimental import pallas as pl
from jax.experimental.pallas import tpu as pltpu
from jax.sharding import PartitionSpec as P

MESH = pl.DeviceIdType.MESH
HIGH = lax.Precision.HIGHEST


def axis_operator(length):
    index = np.arange(length)
    signed = np.where(index < length // 2, index, index - length) * (2.0 * math.pi / length)
    phases = (index[:, None] * index[None, :] % length) * (2.0 * math.pi / length)
    first = (np.cos(phases) @ (0.5 * signed * signed)) / length
    return np.asarray(first[(index[:, None] - index[None, :]) % length], np.float32)


def dot(left, right):
    return jnp.dot(left, right, precision=HIGH, preferred_element_type=jnp.float32)


def lanes(product):
    total = jnp.sum(product, axis=0, keepdims=True)
    return sum(total[:, i : i + 128] for i in range(0, total.shape[1], 128))


def kernel(
    cy, cz, nx, fy, fz,
    states_ref, pot_ref, dx_ref, dy_ref, dz_ref,
    out_ref, corr_ref, energy_ref,
    b_ref, ysend, yb, zb, ymul, zmul, yback, zback, s_ref, u_ref, yusend, yu, zu,
    acc1, acc2, sum1, sum2, part1, part2, part1z, part2z,
    send_sem, recv_sem,
):
    pole, my, mz = lax.axis_index("pole"), lax.axis_index("fy"), lax.axis_index("fz")
    rows = cy * cz
    wide = 2 * nx
    first, second = slice(0, nx), slice(nx, wide)

    def at_y(index):
        return (pole, index, mz)

    def at_z(index):
        return (pole, my, index)

    def chunk(index, size):
        return pl.ds(pl.multiple_of(index * size, size), size)

    def scatter(src, dst, size, count, me, place, slot, broadcast=False):
        def body(step, carry):
            other = lax.rem(me + step, count)
            pltpu.make_async_remote_copy(
                src_ref=src if broadcast else src.at[chunk(other, size)],
                dst_ref=dst.at[chunk(me, size)],
                send_sem=send_sem.at[slot],
                recv_sem=recv_sem.at[slot],
                device_id=place(other),
                device_id_type=MESH,
            ).start()
            return carry

        lax.fori_loop(1, count, body, 0)
        dst[chunk(me, size)] = src[...] if broadcast else src[chunk(me, size)]

    def arrived(dst, size, count, slot):
        whole = dst.at[pl.ds(0, (count - 1) * size)]
        pltpu.make_async_copy(whole, whole, recv_sem.at[slot]).wait()

    def sent(dst, size, count, slot):
        whole = dst.at[pl.ds(0, (count - 1) * size)]
        pltpu.make_async_copy(whole, whole, send_sem.at[slot]).wait()

    barrier = pltpu.get_barrier_semaphore()

    def greet_y(step, carry):
        pl.semaphore_signal(
            barrier, inc=1, device_id=at_y(lax.rem(my + step, fy)), device_id_type=MESH
        )
        return carry

    def greet_z(step, carry):
        pl.semaphore_signal(
            barrier, inc=1, device_id=at_z(lax.rem(mz + step, fz)), device_id_type=MESH
        )
        return carry

    lax.fori_loop(1, fy, greet_y, 0)
    lax.fori_loop(1, fz, greet_z, 0)

    b_ref[:, first] = states_ref[0].reshape(rows, nx)
    b_ref[:, second] = states_ref[1].reshape(rows, nx)

    def swapped(value, major, minor):
        return jnp.swapaxes(value.reshape(major, minor, wide), 0, 1).reshape(rows, wide)

    ysend[...] = swapped(b_ref[...], cy, cz)
    pl.semaphore_wait(barrier, fy + fz - 2)

    scatter(ysend, yb, cy, fy, my, at_y, 0)
    scatter(b_ref, zb, cz, fz, mz, at_z, 1)

    b0, b1 = b_ref[:, first], b_ref[:, second]
    v = pot_ref[...].reshape(rows, nx)
    s_ref[:, first] = v * b0 + dot(b0, dx_ref[...])
    s_ref[:, second] = v * b1 + dot(b1, dx_ref[...])
    acc1[0:1] = lanes(b0 * b0)
    acc1[1:2] = lanes(b0 * b1)
    acc1[2:3] = lanes(b1 * b1)
    acc1[5:8] = jnp.zeros((3, 128), jnp.float32)
    own0 = lanes(b0 * s_ref[:, first])
    own1 = lanes(b1 * s_ref[:, second])

    arrived(zb, cz, fz, 1)
    zmul[...] = dot(dz_ref[...], zb[...])
    scatter(zmul, zback, cz, fz, mz, at_z, 3)
    arrived(yb, cy, fy, 0)
    ymul[...] = dot(dy_ref[...], yb[...])
    scatter(ymul, yback, cy, fy, my, at_y, 2)

    zz = zb[...] * zmul[...]
    yy = yb[...] * ymul[...]
    acc1[3:4] = own0 + lanes(zz[:, first]) + lanes(yy[:, first])
    acc1[4:5] = own1 + lanes(zz[:, second]) + lanes(yy[:, second])
    scatter(acc1, part1, 8, fy, my, at_y, 6, True)

    arrived(zback, cz, fz, 3)
    s_ref[...] += zback[...]
    arrived(part1, 8, fy, 6)
    sum1[...] = sum(part1[8 * i : 8 * i + 8] for i in range(fy))
    scatter(sum1, part1z, 8, fz, mz, at_z, 7, True)
    arrived(yback, cy, fy, 2)
    u_ref[...] = s_ref[...] + swapped(yback[...], cz, cy)
    scatter(u_ref, zu, cz, fz, mz, at_z, 5)
    yusend[...] = swapped(u_ref[...], cy, cz)
    scatter(yusend, yu, cy, fy, my, at_y, 4)

    arrived(part1z, 8, fz, 7)
    total1 = jnp.sum(sum(part1z[8 * i : 8 * i + 8] for i in range(fz)), axis=1, keepdims=True)
    m00, m01, m11 = total1[0:1], total1[1:2], total1[2:3]
    mu0, mu1 = total1[3:4] / m00, total1[4:5] / m11

    w0 = u_ref[:, first] - mu0 * b0
    w1 = u_ref[:, second] - mu1 * b1
    s_ref[:, first] = w0
    s_ref[:, second] = w1
    t0 = v * w0 + dot(w0, dx_ref[...])
    t1 = v * w1 + dot(w1, dx_ref[...])
    acc2[0:1] = lanes(w0 * w0)
    acc2[1:2] = lanes(w0 * w1)
    acc2[2:3] = lanes(w1 * w1)
    acc2[6:7] = lanes(b0 * w0)
    acc2[7:8] = lanes(b0 * w1)
    acc2[8:9] = lanes(b1 * w0)
    acc2[9:10] = lanes(b1 * w1)
    acc2[10:16] = jnp.zeros((6, 128), jnp.float32)
    h00, h01, h11 = lanes(w0 * t0), lanes(w0 * t1), lanes(w1 * t1)

    def quadratic(operator, pencil, base):
        left0 = pencil[:, first] - mu0 * base[:, first]
        left1 = pencil[:, second] - mu1 * base[:, second]
        right0 = dot(operator[...], left0)
        right1 = dot(operator[...], left1)
        return lanes(left0 * right0), lanes(left0 * right1), lanes(left1 * right1)

    arrived(zu, cz, fz, 5)
    z00, z01, z11 = quadratic(dz_ref, zu, zb)
    arrived(yu, cy, fy, 4)
    y00, y01, y11 = quadratic(dy_ref, yu, yb)
    acc2[3:4] = h00 + z00 + y00
    acc2[4:5] = h01 + z01 + y01
    acc2[5:6] = h11 + z11 + y11

    scatter(acc2, part2, 16, fy, my, at_y, 8, True)
    arrived(part2, 16, fy, 8)
    sum2[...] = sum(part2[16 * i : 16 * i + 16] for i in range(fy))
    scatter(sum2, part2z, 16, fz, mz, at_z, 9, True)
    arrived(part2z, 16, fz, 9)
    total2 = jnp.sum(sum(part2z[16 * i : 16 * i + 16] for i in range(fz)), axis=1, keepdims=True)
    w00, w01, w11, e00, e01, e11, c00, c01, c10, c11 = (total2[i : i + 1] for i in range(10))

    def factors(mu, norm, ww, whw):
        nu = jnp.where(ww > 0.0, whw / jnp.where(ww > 0.0, ww, 1.0), mu)
        t2 = ww / norm
        p, q = mu - 1.0, nu - 1.0
        trace, det = p + q, p * q - t2
        real, imag = det * det - 1.0, 2.0 * det - trace * trace
        size = real * real + imag * imag
        return ((det - q * trace) * imag - real) / size, trace * imag / size

    a0, f0 = factors(mu0, m00, w00, e00)
    a1, f1 = factors(mu1, m11, w11, e11)
    own = pole == 0
    out = jnp.where(own, a0, a1) * jnp.where(own, b0, b1) + jnp.where(own, f0, f1) * jnp.where(
        own, w0, w1
    )
    out_ref[0] = out.reshape(cy, cz, nx)

    cells = 1.0 / float(nx * cy * fy * cz * fz)

    def correlation(ai, fi, aj, fj, bb, biwj, bjwi, ww):
        return (ai * aj * bb + ai * fj * biwj + fi * aj * bjwi + fi * fj * ww) * cells

    def energy(ai, fi, aj, fj, mui, muj, bb, biwj, bjwi, ww, whw):
        bhb = biwj + muj * bb
        bihwj = ww + mui * biwj
        wihbj = ww + muj * bjwi
        return (ai * aj * bhb + ai * fj * bihwj + fi * aj * wihbj + fi * fj * whw) * cells

    cross = correlation(a0, f0, a1, f1, m01, c01, c10, w01)
    corr_ref[0:1, 0:1] = correlation(a0, f0, a0, f0, m00, c00, c00, w00)
    corr_ref[0:1, 1:2] = cross
    corr_ref[1:2, 0:1] = cross
    corr_ref[1:2, 1:2] = correlation(a1, f1, a1, f1, m11, c11, c11, w11)
    cross = energy(a0, f0, a1, f1, mu0, mu1, m01, c01, c10, w01, e01)
    energy_ref[0:1, 0:1] = energy(a0, f0, a0, f0, mu0, mu0, m00, c00, c00, w00, e00)
    energy_ref[0:1, 1:2] = cross
    energy_ref[1:2, 0:1] = cross
    energy_ref[1:2, 1:2] = energy(a1, f1, a1, f1, mu1, mu1, m11, c11, c11, w11, e11)

    sent(yb, cy, fy, 0)
    sent(zb, cz, fz, 1)
    sent(yback, cy, fy, 2)
    sent(zback, cz, fz, 3)
    sent(yu, cy, fy, 4)
    sent(zu, cz, fz, 5)
    sent(part1, 8, fy, 6)
    sent(part1z, 8, fz, 7)
    sent(part2, 16, fy, 8)
    sent(part2z, 16, fz, 9)


def local(states, potential):
    columns, cy, cz, nx = states.shape
    fy, fz = lax.axis_size("fy"), lax.axis_size("fz")
    rows = cy * cz
    block = pltpu.VMEM((rows, columns * nx), jnp.float32)
    f32 = jnp.float32
    in_vmem = pl.BlockSpec(memory_space=pltpu.VMEM)
    return pl.pallas_call(
        functools.partial(kernel, cy, cz, nx, fy, fz),
        out_shape=(
            jax.ShapeDtypeStruct((1, cy, cz, nx), f32),
            jax.ShapeDtypeStruct((columns, columns), f32),
            jax.ShapeDtypeStruct((columns, columns), f32),
        ),
        in_specs=[in_vmem] * 5,
        out_specs=(in_vmem,) * 3,
        scratch_shapes=[block] * 13
        + [
            pltpu.VMEM((8, 128), f32),
            pltpu.VMEM((16, 128), f32),
            pltpu.VMEM((8, 128), f32),
            pltpu.VMEM((16, 128), f32),
            pltpu.VMEM((8 * fy, 128), f32),
            pltpu.VMEM((16 * fy, 128), f32),
            pltpu.VMEM((8 * fz, 128), f32),
            pltpu.VMEM((16 * fz, 128), f32),
            pltpu.SemaphoreType.DMA((10,)),
            pltpu.SemaphoreType.DMA((10,)),
        ],
        compiler_params=pltpu.CompilerParams(
            collective_id=0, has_side_effects=True, vmem_limit_bytes=32 * 1024 * 1024
        ),
    )(
        states,
        potential,
        jnp.asarray(axis_operator(nx)),
        jnp.asarray(axis_operator(cy * fy)),
        jnp.asarray(axis_operator(cz * fz)),
    )


def solution(mesh):
    placed = (P(None, "fy", "fz", None), P("fy", "fz", None))
    return jax.shard_map(
        local,
        mesh=mesh,
        in_specs=placed,
        out_specs=(P("pole", "fy", "fz", None), P(), P()),
        check_vma=False,
    )
```

time: 1500 us -> 52.1 us (0.03)
  blocking collectives: 1110 us -> 0 us
  waiting for transfers between devices: 153 us -> 0 us
  starting transfers between devices: 102 us -> 0 us
  matrix products: 93.8 us -> 0 us
  Pallas kernels: 0 us -> 45.8 us
  local copies, waits for them, and re-layouts: 21.1 us -> 5.42 us
    psum x4 -> x0, blocking collectives: 1110 us -> none  [the longest x3 833 us: summed(): return lax.psum((values[0], values[1]), ('fy', 'fz'))]
    all_to_all x20 -> x0, waiting for transfers between devices: 119 us -> none  [the longest x5 37 us: across_y(): lax.all_to_all(fields[1], 'fy', split_axis=1, concat_axis=2, tiled=True)]
    all_to_all x20 -> x0, starting transfers between devices: 102 us -> none  [the longest x5 31.3 us: across_z(): lax.all_to_all(fields[0], 'fz', split_axis=1, concat_axis=2, tiled=True)]
    dot_general x58 -> x0, matrix products: 93.8 us -> none  [the longest x54 83.7 us: product(): return jnp.einsum(pattern, operand, matrix, precision=lax.Precision.HIGHEST)]
    pallas_call x0 -> x1, Pallas kernels: none -> 45.8 us  [local(): pl.pallas_call(functools.partial(kernel, cy, cz, nx, fy, fz), out_shape=(...]
    psum x1 -> x0, waiting for transfers between devices: 33.5 us -> none  [local(): filter_block = lax.psum(contribution, 'pole')]
    reshape x30 -> x0, local copies, waits for them, and re-layouts: 17.9 us -> none  [reshaped(): return (fields[0].reshape(shape), fields[1].reshape(shape))]
  transfers between devices with their start and end apart: 21 -> 0, of which waited for: 21 -> 0; matrix products, arithmetic and copies ran while one was open for 3% -> 0% of each run, Pallas kernels for 0% -> 0%
where the time goes in v1:
time: 52.1 us; the launch traced here: 51.9 us
  Pallas kernels  45.8 us (88%)
  local copies, waits for them, and re-layouts  5.42 us (10%)
  between operations  0.65 us (1%)
    pallas_call x1, Pallas kernels, local(): pl.pallas_call(functools.partial(kernel, cy, cz, nx, fy, fz), out_shape=(...  45.8 us
    unnamed x11, local copies, waits for them, and re-layouts  5.42 us

profile of v1, /device:TPU:1, one launch (start us, length us, event | category | flops | bytes accessed | tf_op | source)
XLA Modules:
  0.0 51.9 jit_solution(7582716073778694885)
XLA Ops:
  0.6 0.0 copy-start
  0.6 0.9 %copy-done = f32[2,16,8,256]{3,2,1,0:T(8,128)S(1)} copy-done((f32[2,16,8,256]{3,2,1,0:T(8,128)S(1)}, f32[2,16,8,256]{3,2,1,0:T(8,128)}, u32[]{:S(2)}) %copy-start) | copy-done | bytes 262168
  1.6 0.0 copy-start.1
  1.6 0.9 %copy-done.1 = f32[256,256]{1,0:T(8,128)S(1)} copy-done((f32[256,256]{1,0:T(8,128)S(1)}, f32[256,256]{1,0:T(8,128)}, u32[]{:S(2)}) %copy-start.1) | copy-done | bytes 262168
  2.5 0.0 copy-start.2
  2.5 0.8 %copy-done.2 = f32[128,128]{1,0:T(8,128)S(1)} copy-done((f32[128,128]{1,0:T(8,128)S(1)}, f32[128,128]{1,0:T(8,128)}, u32[]{:S(2)}) %copy-start.2) | copy-done | bytes 65560
  3.4 0.0 copy-start.3
  3.4 0.9 %copy-done.3 = f32[16,8,256]{2,1,0:T(8,128)S(1)} copy-done((f32[16,8,256]{2,1,0:T(8,128)S(1)}, f32[16,8,256]{2,1,0:T(8,128)}, u32[]{:S(2)}) %copy-start.3) | copy-done | bytes 131096
  4.3 45.8 %shard_map.76 = (f32[1,16,8,256]{3,2,1,0:T(8,128)S(1)}, f32[2,2]{1,0:T(2,128)S(1)}, f32[2,2]{1,0:T(2,128)S(1)}) custom-call(f32[2,16,8,256]{3,2,1,0:T(8,128)S(1)} %copy-done, f32[16,8,256]{2,1,0:T(8,128)S(1)} %copy-done.3, f32[256,256]{1,0:T(8,128)S(1)} %copy-done.1, f32[128,128]{1,0:T(8,128)S(1)} %copy-done.2, f32[128,128]{1,0:T(8,128)S(1)} %copy-done.2), custom_call_target="tpu_custom_call" | custom-call | tf_op jit(solution)/shard_map/pallas_call | solution.py:245
  50.1 0.7 %copy.11 = f32[1,16,8,256]{3,2,1,0:T(8,128)} copy(f32[1,16,8,256]{3,2,1,0:T(8,128)S(1)} %get-tuple-element.6) | data formatting | bytes 262144
  50.7 0.6 %copy.12 = f32[2,2]{1,0:T(2,128)} copy(f32[2,2]{1,0:T(2,128)S(1)} %get-tuple-element.7) | data formatting | bytes 32
  51.3 0.6 %copy.13 = f32[2,2]{1,0:T(2,128)} copy(f32[2,2]{1,0:T(2,128)S(1)} %get-tuple-element.8) | data formatting | bytes 32
Async XLA Ops:
  0.6 1.0 %copy-start = (f32[2,16,8,256]{3,2,1,0:T(8,128)S(1)}, f32[2,16,8,256]{3,2,1,0:T(8,128)}, u32[]{:S(2)}) copy-start(f32[2,16,8,256]{3,2,1,0:T(8,128)} %states_ref.1) | copy-start | bytes 786436
  1.6 0.9 %copy-start.1 = (f32[256,256]{1,0:T(8,128)S(1)}, f32[256,256]{1,0:T(8,128)}, u32[]{:S(2)}) copy-start(f32[256,256]{1,0:T(8,128)} %constant.4.clone.dx_ref) | copy-start | bytes 786436
  2.5 0.8 %copy-start.2 = (f32[128,128]{1,0:T(8,128)S(1)}, f32[128,128]{1,0:T(8,128)}, u32[]{:S(2)}) copy-start(f32[128,128]{1,0:T(8,128)} %constant.5.clone.dy_ref.dz_ref) | copy-start | bytes 196612
  3.4 0.9 %copy-start.3 = (f32[16,8,256]{2,1,0:T(8,128)S(1)}, f32[16,8,256]{2,1,0:T(8,128)}, u32[]{:S(2)}) copy-start(f32[16,8,256]{2,1,0:T(8,128)} %pot_ref.1) | copy-start | bytes 393220

commit v2 on v1

v2 whole, which is shorter than its diff:
```python
import functools
import math

import jax
import jax.numpy as jnp
import numpy as np
from jax import lax
from jax.experimental import pallas as pl
from jax.experimental.pallas import tpu as pltpu
from jax.sharding import PartitionSpec as P

MESH = pl.DeviceIdType.MESH
HIGH = lax.Precision.HIGHEST


def axis_operator(length):
    index = np.arange(length)
    signed = np.where(index < length // 2, index, index - length) * (2.0 * math.pi / length)
    phases = (index[:, None] * index[None, :] % length) * (2.0 * math.pi / length)
    first = (np.cos(phases) @ (0.5 * signed * signed)) / length
    return np.asarray(first[(index[:, None] - index[None, :]) % length], np.float32)


def far_first(count):
    return sorted(range(1, count), key=lambda k: -min(k, count - k))


def dot(left, right):
    return jnp.dot(left, right, precision=HIGH, preferred_element_type=jnp.float32)


def lanes(product):
    return jnp.sum(product, axis=0, keepdims=True)


def kernel(
    cy, cz, nx, fy, fz, poles,
    states_hbm, pot_hbm, dx_hbm, dy_hbm, dz_hbm,
    w_ref, coef_ref, corr_ref, energy_ref,
    own_b, far_b, v_ref, dx_ref, dy_ref, dz_ref, s_ref, u_ref,
    ysend, yb, zb, ymul, zmul, yback, zback, yusend, yu, zu, far_u, far_w,
    acc1, acc2, sum1, sum2, part1, part2, part1z, part2z,
    load_sem, send_sem, recv_sem,
):
    pole, my, mz = lax.axis_index("pole"), lax.axis_index("fy"), lax.axis_index("fz")
    partner = 1 - pole
    plane = pole * fz + mz
    rows = cy * cz
    half = nx // 2
    split = cy // 2
    col0, col1 = slice(0, half), slice(half, nx)

    def lane_block(index):
        return pl.ds(pl.multiple_of(index * half, half), half)

    def at_y(step):
        return (pole, lax.rem(my + step, fy), mz)

    def at_z(step):
        return (pole, my, lax.rem(mz + step, fz))

    def at_plane(step):
        other = lax.rem(plane + step, poles * fz)
        return (other // fz, my, lax.rem(other, fz))

    def push(src, dst, place, slot):
        pltpu.make_async_remote_copy(
            src_ref=src,
            dst_ref=dst,
            send_sem=send_sem.at[slot],
            recv_sem=recv_sem.at[slot],
            device_id=place,
            device_id_type=MESH,
        ).start()

    def push_y(src, dst, step, slot):
        push(src.at[lax.rem(my + step, fy)], dst.at[my], at_y(step), slot)

    def push_z(src, dst, step, slot):
        push(src.at[lax.rem(mz + step, fz)], dst.at[mz], at_z(step), slot)

    def exchange(ysrc, ydst, yslot, zsrc, zdst, zslot):
        ysteps, zsteps = far_first(fy), far_first(fz)
        for i in range(max(fy, fz) - 1):
            if i < len(ysteps):
                push_y(ysrc, ydst, ysteps[i], yslot)
            if i < len(zsteps):
                push_z(zsrc, zdst, zsteps[i], zslot)
        ydst[my] = ysrc[my]
        zdst[mz] = zsrc[mz]

    def spread(src, dst, count, me, place, slot):
        def body(step, carry):
            push(src, dst.at[me], place(step), slot)
            return carry

        lax.fori_loop(1, count, body, 0)
        dst[me] = src[...]

    def arrived(dst, count, slot):
        whole = dst.at[pl.ds(0, count)]
        pltpu.make_async_copy(whole, whole, recv_sem.at[slot]).wait()

    def sent(dst, count, slot):
        whole = dst.at[pl.ds(0, count)]
        pltpu.make_async_copy(whole, whole, send_sem.at[slot]).wait()

    barrier = pltpu.get_barrier_semaphore()

    def greet(count, place):
        def body(step, carry):
            pl.semaphore_signal(barrier, inc=1, device_id=place(step), device_id_type=MESH)
            return carry

        lax.fori_loop(1, count, body, 0)

    greet(fy, at_y)
    greet(poles * fz, at_plane)

    def load(src, dst, slot):
        copy = pltpu.make_async_copy(src, dst, load_sem.at[slot])
        copy.start()
        return copy

    near = [load(states_hbm.at[c, :, :, lane_block(pole)], own_b.at[:, :, pl.ds(c * half, half)], c) for c in range(2)]
    rest = [
        load(states_hbm.at[c, :, :, lane_block(partner)], far_b.at[:, :, pl.ds(c * half, half)], 2 + c) for c in range(2)
    ]
    rest.append(load(pot_hbm.at[:, :, lane_block(pole)], v_ref, 4))
    rest.append(load(dx_hbm, dx_ref, 5))
    rest.append(load(dz_hbm, dz_ref, 6))
    rest.append(load(dy_hbm, dy_ref, 7))
    for copy in near:
        copy.wait()
    ysend[...] = jnp.swapaxes(own_b[...], 0, 1)
    pl.semaphore_wait(barrier, fy + poles * fz - 2)

    exchange(ysend, yb, 0, own_b, zb, 1)
    for copy in rest:
        copy.wait()

    def flat(ref):
        return ref[...].reshape(rows, nx)

    def column(ref, c):
        return ref[:, :, c * half : (c + 1) * half].reshape(-1, half)

    v = v_ref[...].reshape(rows, half)
    b = [column(own_b, c) for c in range(2)]
    s = []
    for c in range(2):
        whole = jnp.concatenate([b[c], column(far_b, c)], axis=1)
        s.append(v * b[c] + dot(whole, dx_ref[:, col0]))
        s_ref[:, :, c * half : (c + 1) * half] = s[c].reshape(cy, cz, half)
    acc1[0:1] = lanes(b[0] * b[0])
    acc1[1:2] = lanes(b[0] * b[1])
    acc1[2:3] = lanes(b[1] * b[1])
    acc1[5:8] = jnp.zeros((3, 128), jnp.float32)
    own = [lanes(b[c] * s[c]) for c in range(2)]

    arrived(zb, fz - 1, 1)
    zmul[...] = dot(dz_ref[...], flat(zb)).reshape(fz, cz, nx)
    for step in far_first(fz):
        push_z(zmul, zback, step, 3)
    zback[mz] = zmul[mz]
    arrived(yb, fy - 1, 0)
    ymul[...] = dot(dy_ref[...], flat(yb)).reshape(fy, cy, nx)
    for step in far_first(fy):
        push_y(ymul, yback, step, 2)
    yback[my] = ymul[my]

    both = lanes(flat(zb) * flat(zmul)) + lanes(flat(yb) * flat(ymul))
    acc1[3:4] = own[0] + both[:, col0]
    acc1[4:5] = own[1] + both[:, col1]
    spread(acc1, part1, fy, my, at_y, 6)

    arrived(zback, fz - 1, 3)
    s_ref[...] += zback[...]
    arrived(part1, fy - 1, 6)
    sum1[...] = jnp.sum(part1[...], axis=0)
    spread(sum1, part1z, poles * fz, plane, at_plane, 7)
    arrived(yback, fy - 1, 2)
    u_ref[...] = s_ref[...] + jnp.swapaxes(yback[...], 0, 1)
    yusend[...] = jnp.swapaxes(u_ref[...], 0, 1)
    exchange(yusend, yu, 4, u_ref, zu, 5)
    across = (partner, my, mz)
    push(u_ref.at[pl.ds(partner * split, split)], far_u, across, 10)
    push(u_ref.at[pl.ds(pole * split, split), :, lane_block(partner)], far_w, across, 11)

    arrived(part1z, poles * fz - 1, 7)
    total1 = jnp.sum(jnp.sum(part1z[...], axis=0), axis=1, keepdims=True)
    m00, m01, m11 = total1[0:1], total1[1:2], total1[2:3]
    mu = [total1[3:4] / m00, total1[4:5] / m11]

    w = [column(u_ref, c) - mu[c] * b[c] for c in range(2)]
    acc2[0:1] = lanes(w[0] * w[0])
    acc2[1:2] = lanes(w[0] * w[1])
    acc2[2:3] = lanes(w[1] * w[1])
    acc2[6:7] = lanes(b[0] * w[1])
    acc2[7:8] = lanes(b[1] * w[0])
    applied = [v * w[0], v * w[1]]
    terms = [lanes(w[0] * applied[0]), lanes(w[0] * applied[1]), lanes(w[1] * applied[1])]

    def quadratic(left, right):
        terms[0] += lanes(left[0] * right[0])
        terms[1] += lanes(left[0] * right[1])
        terms[2] += lanes(left[1] * right[1])

    arrived(far_u, split, 10)
    mine = pl.ds(pole * split, split)
    whole = []
    for c in range(2):
        block = slice(c * half, (c + 1) * half)
        near_part = u_ref[mine, :, block] - mu[c] * own_b[mine, :, block]
        far_part = far_u[:, :, block] - mu[c] * far_b[mine, :, block]
        whole.append(jnp.concatenate([near_part, far_part], axis=2).reshape(split * cz, nx))
    product = [dot(whole[c], dx_ref[...]) for c in range(2)]
    x_terms = [lanes(whole[0] * product[0]), lanes(whole[0] * product[1]), lanes(whole[1] * product[1])]
    for i in range(3):
        terms[i] = terms[i] + x_terms[i][:, col0] + x_terms[i][:, col1]

    def pencil(operator, u_pencil, b_pencil):
        left = [column(u_pencil, c) - mu[c] * column(b_pencil, c) for c in range(2)]
        quadratic(left, [dot(operator[...], left[c]) for c in range(2)])

    arrived(zu, fz - 1, 5)
    pencil(dz_ref, zu, zb)
    arrived(yu, fy - 1, 4)
    pencil(dy_ref, yu, yb)
    for i in range(3):
        acc2[3 + i : 4 + i] = terms[i]

    spread(acc2, part2, fy, my, at_y, 8)

    first = pole == 0
    my_mu = jnp.where(first, mu[0], mu[1])
    w_ref[0, :, :, lane_block(pole)] = jnp.where(first, w[0], w[1]).reshape(cy, cz, half)
    arrived(far_w, split, 11)
    others = pl.ds(partner * split, split)
    w_ref[0, mine, :, lane_block(partner)] = far_u[:, :, lane_block(pole)] - my_mu * far_b[mine, :, lane_block(pole)]
    w_ref[0, others, :, lane_block(partner)] = far_w[...] - my_mu * far_b[others, :, lane_block(pole)]

    arrived(part2, fy - 1, 8)
    sum2[...] = jnp.sum(part2[...], axis=0)
    spread(sum2, part2z, poles * fz, plane, at_plane, 9)

    sent(yb, fy - 1, 0)
    sent(zb, fz - 1, 1)
    sent(yback, fy - 1, 2)
    sent(zback, fz - 1, 3)
    sent(yu, fy - 1, 4)
    sent(zu, fz - 1, 5)
    sent(part1, fy - 1, 6)
    sent(part1z, poles * fz - 1, 7)
    sent(part2, fy - 1, 8)
    sent(far_u, split, 10)
    sent(far_w, split, 11)

    arrived(part2z, poles * fz - 1, 9)
    total2 = jnp.sum(jnp.sum(part2z[...], axis=0), axis=1, keepdims=True)
    w00, w01, w11, e00, e01, e11, c01, c10 = (total2[i : i + 1] for i in range(8))

    def factors(mean, norm, ww, whw):
        nu = jnp.where(ww > 0.0, whw / jnp.where(ww > 0.0, ww, 1.0), mean)
        t2 = ww / norm
        p, q = mean - 1.0, nu - 1.0
        trace, det = p + q, p * q - t2
        real, imag = det * det - 1.0, 2.0 * det - trace * trace
        size = real * real + imag * imag
        return ((det - q * trace) * imag - real) / size, trace * imag / size

    a0, f0 = factors(mu[0], m00, w00, e00)
    a1, f1 = factors(mu[1], m11, w11, e11)
    coef_ref[0:1] = jnp.broadcast_to(jnp.where(first, a0, a1), (1, 128))
    coef_ref[1:2] = jnp.broadcast_to(jnp.where(first, f0, f1), (1, 128))

    corr_ref[0:1, 0:1] = a0 * a0 * m00 + f0 * f0 * w00
    corr_ref[1:2, 1:2] = a1 * a1 * m11 + f1 * f1 * w11
    cross = a0 * a1 * m01 + a0 * f1 * c01 + f0 * a1 * c10 + f0 * f1 * w01
    corr_ref[0:1, 1:2] = cross
    corr_ref[1:2, 0:1] = cross
    energy_ref[0:1, 0:1] = a0 * a0 * mu[0] * m00 + 2.0 * a0 * f0 * w00 + f0 * f0 * e00
    energy_ref[1:2, 1:2] = a1 * a1 * mu[1] * m11 + 2.0 * a1 * f1 * w11 + f1 * f1 * e11
    cross = (
        a0 * a1 * (c01 + mu[1] * m01)
        + a0 * f1 * (w01 + mu[0] * c01)
        + f0 * a1 * (w01 + mu[1] * c10)
        + f0 * f1 * e01
    )
    energy_ref[0:1, 1:2] = cross
    energy_ref[1:2, 0:1] = cross
    sent(part2z, poles * fz - 1, 9)


def local(states, potential):
    columns, cy, cz, nx = states.shape
    fy, fz, poles = lax.axis_size("fy"), lax.axis_size("fz"), lax.axis_size("pole")
    half = nx // 2
    f32 = jnp.float32
    in_vmem = pl.BlockSpec(memory_space=pltpu.VMEM)
    in_hbm = pl.BlockSpec(memory_space=pl.ANY)

    def vmem(*shape):
        return pltpu.VMEM(shape, f32)

    x_block, y_block = vmem(cy, cz, nx), vmem(fy, cy, nx)
    sums = vmem(8, 128)
    w, coef, corr, energy = pl.pallas_call(
        functools.partial(kernel, cy, cz, nx, fy, fz, poles),
        out_shape=(
            jax.ShapeDtypeStruct((1, cy, cz, nx), f32),
            jax.ShapeDtypeStruct((8, 128), f32),
            jax.ShapeDtypeStruct((columns, columns), f32),
            jax.ShapeDtypeStruct((columns, columns), f32),
        ),
        in_specs=[in_hbm] * 5,
        out_specs=(in_vmem,) * 4,
        scratch_shapes=[
            x_block, x_block, vmem(cy, cz, half),
            vmem(nx, nx), vmem(cy * fy, cy * fy), vmem(cz * fz, cz * fz),
            x_block, x_block,
            y_block, y_block, vmem(fz, cz, nx),
            y_block, vmem(fz, cz, nx), y_block, vmem(fz, cz, nx),
            y_block, y_block, vmem(fz, cz, nx),
            vmem(cy // 2, cz, nx), vmem(cy // 2, cz, half),
            sums, sums, sums, sums,
            vmem(fy, 8, 128), vmem(fy, 8, 128), vmem(poles * fz, 8, 128), vmem(poles * fz, 8, 128),
            pltpu.SemaphoreType.DMA((8,)),
            pltpu.SemaphoreType.DMA((12,)),
            pltpu.SemaphoreType.DMA((12,)),
        ],
        compiler_params=pltpu.CompilerParams(
            collective_id=0, has_side_effects=True, vmem_limit_bytes=62 * 1024 * 1024
        ),
    )(
        states,
        potential,
        jnp.asarray(axis_operator(nx)),
        jnp.asarray(axis_operator(cy * fy)),
        jnp.asarray(axis_operator(cz * fz)),
    )
    mine = lax.dynamic_slice_in_dim(states, lax.axis_index("pole"), 1, 0)
    cells = 1.0 / float(nx * cy * fy * cz * fz)
    return coef[0, 0] * mine + coef[1, 0] * w, corr * cells, energy * cells


def solution(mesh):
    placed = (P(None, "fy", "fz", None), P("fy", "fz", None))
    return jax.shard_map(
        local,
        mesh=mesh,
        in_specs=placed,
        out_specs=(P("pole", "fy", "fz", None), P(), P()),
        check_vma=False,
    )
```

time: 52.1 us -> 46.6 us (0.89)
  Pallas kernels: 45.8 us -> 41.1 us
  local copies, waits for them, and re-layouts: 5.42 us -> 1.28 us
  other arithmetic: 0 us -> 3.44 us
    unnamed x11 -> x6, local copies, waits for them, and re-layouts: 5.42 us -> 0.01 us
    pallas_call x1, Pallas kernels: 45.8 us -> 41.1 us  [local(): pl.pallas_call(functools.partial(kernel, cy, cz, nx, fy, fz, poles), out_...]
    add x0 -> x1, other arithmetic: none -> 2.87 us  [local(): return (coef[0, 0] * mine + coef[1, 0] * w, corr * cells, energy * cells)]
    slice x0 -> x1, local copies, waits for them, and re-layouts: none -> 1.27 us  [local(): return (coef[0, 0] * mine + coef[1, 0] * w, corr * cells, energy * cells)]
    mul x0 -> x1, other arithmetic: none -> 0.57 us  [local(): return (coef[0, 0] * mine + coef[1, 0] * w, corr * cells, energy * cells)]
where the time goes in v2:
time: 46.6 us; the launch traced here: 46.5 us
  Pallas kernels  41.1 us (88%)
  other arithmetic  3.44 us (7%)
  local copies, waits for them, and re-layouts  1.28 us (3%)
  between operations  0.66 us (1%)
    pallas_call x1, Pallas kernels, local(): pl.pallas_call(functools.partial(kernel, cy, cz, nx, fy, fz, poles), out_...  41.1 us
    add x1, other arithmetic, local(): return (coef[0, 0] * mine + coef[1, 0] * w, corr * cells, energy * cells)  2.87 us
    slice x1, local copies, waits for them, and re-layouts, local(): return (coef[0, 0] * mine + coef[1, 0] * w, corr * cells, energy * cells)  1.27 us

profile of v2, /device:TPU:1, one launch (start us, length us, event | category | flops | bytes accessed | tf_op | source)
XLA Modules:
  0.0 46.5 jit_solution(15494740418556004070)
XLA Ops:
  0.6 0.0 copy-start
  0.6 41.1 %shard_map.76 = (f32[1,16,8,256]{3,2,1,0:T(8,128)}, f32[8,128]{1,0:T(8,128)}, f32[2,2]{1,0:T(2,128)}, f32[2,2]{1,0:T(2,128)}) custom-call(f32[2,16,8,256]{3,2,1,0:T(8,128)} %states_hbm.1, f32[16,8,256]{2,1,0:T(8,128)} %pot_hbm.1, f32[256,256]{1,0:T(8,128)} %constant.16.clone.dx_hbm, f32[128,128]{1,0:T(8,128)} %constant.17.clone.dy_hbm.dz_hbm, ...), custom_call_target="tpu_custom_call" | custom-call | tf_op jit(solution)/shard_map/pallas_call | solution.py:308
  41.7 1.3 %fusion = (f32[1,1]{1,0:T(1,128)}, f32[1,1]{1,0:T(1,128)}) fusion(f32[8,128]{1,0:T(8,128)} %get-tuple-element.7), kind=kLoop, calls=%fused_computation.3 | loop fusion | bytes 16 | tf_op jit(solution)/shard_map/slice | solution.py:344
  43.0 0.0 copy-done
  43.0 0.0 copy-start.1
  43.0 0.0 copy-start.2
  43.0 2.9 %multiply_add_fusion = f32[1,16,8,256]{3,2,1,0:T(8,128)} fusion(f32[1,16,8,256]{3,2,1,0:T(8,128)} %get-tuple-element.8, f32[2,16,8,256]{3,2,1,0:T(8,128)S(1)} %copy-done, s32[]{:T(128)S(6)} %select_n.3, f32[]{:T(128)} %bitcast.1, f32[]{:T(128)} %bitcast), kind=kLoop, calls=%fused_computation | loop fusion | flops 98304 | bytes 393228 | tf_op jit(solution)/shard_map/add | solution.py:344
  45.9 0.0 copy-done.1
  45.9 0.0 copy-done.2
  45.9 0.6 %broadcast_multiply_fusion = (f32[2,2]{1,0:T(2,128)}, f32[2,2]{1,0:T(2,128)}) fusion(f32[2,2]{1,0:T(2,128)S(1)} %copy-done.2, f32[2,2]{1,0:T(2,128)S(1)} %copy-done.1), kind=kLoop, calls=%fused_computation.1 | loop fusion | flops 8 | bytes 64 | tf_op jit(solution)/shard_map/mul | solution.py:344
Async XLA Ops:
  0.6 42.4 %copy-start = (f32[2,16,8,256]{3,2,1,0:T(8,128)S(1)}, f32[2,16,8,256]{3,2,1,0:T(8,128)}, u32[]{:S(2)}) copy-start(f32[2,16,8,256]{3,2,1,0:T(8,128)} %states_hbm.1) | copy-start | bytes 786436
  43.0 2.9 %copy-start.1 = (f32[2,2]{1,0:T(2,128)S(1)}, f32[2,2]{1,0:T(2,128)}, u32[]{:S(2)}) copy-start(f32[2,2]{1,0:T(2,128)} %get-tuple-element.9) | copy-start | bytes 52
  43.0 2.9 %copy-start.2 = (f32[2,2]{1,0:T(2,128)S(1)}, f32[2,2]{1,0:T(2,128)}, u32[]{:S(2)}) copy-start(f32[2,2]{1,0:T(2,128)} %get-tuple-element.10) | copy-start | bytes 52

commit v3 on v2

--- a/solution.py
+++ b/solution.py
@@ -36,10 +36,10 @@
 def kernel(
     cy, cz, nx, fy, fz, poles,
     states_hbm, pot_hbm, dx_hbm, dy_hbm, dz_hbm,
-    w_ref, coef_ref, corr_ref, energy_ref,
+    out_ref, corr_ref, energy_ref,
     own_b, far_b, v_ref, dx_ref, dy_ref, dz_ref, s_ref, u_ref,
-    ysend, yb, zb, ymul, zmul, yback, zback, yusend, yu, zu, far_u, far_w,
-    acc1, acc2, sum1, sum2, part1, part2, part1z, part2z,
+    ysend, yb, zb, ymul, zmul, yback, zback, yusend, yu, zu, far_u, far_w, w_ref,
+    acc1, acc2, sum1, sum2, all1, all2, part1, part2, part1z, part2z,
     load_sem, send_sem, recv_sem,
 ):
     pole, my, mz = lax.axis_index("pole"), lax.axis_index("fy"), lax.axis_index("fz")
@@ -105,17 +105,19 @@
         whole = dst.at[pl.ds(0, count)]
         pltpu.make_async_copy(whole, whole, send_sem.at[slot]).wait()
 
+    def totals(parts, buffer, count):
+        whole = jnp.sum(jnp.sum(parts[...], axis=0), axis=1, keepdims=True)
+        buffer[...] = jnp.broadcast_to(whole, (8, 128))
+        return [buffer[i : i + 1] for i in range(count)]
+
     barrier = pltpu.get_barrier_semaphore()
 
-    def greet(count, place):
-        def body(step, carry):
-            pl.semaphore_signal(barrier, inc=1, device_id=place(step), device_id_type=MESH)
-            return carry
-
-        lax.fori_loop(1, count, body, 0)
-
-    greet(fy, at_y)
-    greet(poles * fz, at_plane)
+    for step in far_first(fy):
+        pl.semaphore_signal(barrier, inc=1, device_id=at_y(step), device_id_type=MESH)
+    for step in far_first(fz):
+        pl.semaphore_signal(barrier, inc=1, device_id=at_z(step), device_id_type=MESH)
+    across = (partner, my, mz)
+    pl.semaphore_signal(barrier, inc=1, device_id=across, device_id_type=MESH)
 
     def load(src, dst, slot):
         copy = pltpu.make_async_copy(src, dst, load_sem.at[slot])
@@ -133,7 +135,7 @@
     for copy in near:
         copy.wait()
     ysend[...] = jnp.swapaxes(own_b[...], 0, 1)
-    pl.semaphore_wait(barrier, fy + poles * fz - 2)
+    pl.semaphore_wait(barrier, fy + fz - 1)
 
     exchange(ysend, yb, 0, own_b, zb, 1)
     for copy in rest:
@@ -176,21 +178,19 @@
 
     arrived(zback, fz - 1, 3)
     s_ref[...] += zback[...]
+    arrived(yback, fy - 1, 2)
+    u_ref[...] = s_ref[...] + jnp.swapaxes(yback[...], 0, 1)
+    yusend[...] = jnp.swapaxes(u_ref[...], 0, 1)
+    push(u_ref.at[pl.ds(partner * split, split)], far_u, across, 10)
+    exchange(yusend, yu, 4, u_ref, zu, 5)
     arrived(part1, fy - 1, 6)
     sum1[...] = jnp.sum(part1[...], axis=0)
     spread(sum1, part1z, poles * fz, plane, at_plane, 7)
-    arrived(yback, fy - 1, 2)
-    u_ref[...] = s_ref[...] + jnp.swapaxes(yback[...], 0, 1)
-    yusend[...] = jnp.swapaxes(u_ref[...], 0, 1)
-    exchange(yusend, yu, 4, u_ref, zu, 5)
-    across = (partner, my, mz)
-    push(u_ref.at[pl.ds(partner * split, split)], far_u, across, 10)
     push(u_ref.at[pl.ds(pole * split, split), :, lane_block(partner)], far_w, across, 11)
 
     arrived(part1z, poles * fz - 1, 7)
-    total1 = jnp.sum(jnp.sum(part1z[...], axis=0), axis=1, keepdims=True)
-    m00, m01, m11 = total1[0:1], total1[1:2], total1[2:3]
-    mu = [total1[3:4] / m00, total1[4:5] / m11]
+    m00, m01, m11, h00, h11 = totals(part1z, all1, 5)
+    mu = [h00 / m00, h11 / m11]
 
     w = [column(u_ref, c) - mu[c] * b[c] for c in range(2)]
     acc2[0:1] = lanes(w[0] * w[0])
@@ -234,11 +234,11 @@
 
     first = pole == 0
     my_mu = jnp.where(first, mu[0], mu[1])
-    w_ref[0, :, :, lane_block(pole)] = jnp.where(first, w[0], w[1]).reshape(cy, cz, half)
+    w_ref[:, :, lane_block(pole)] = jnp.where(first, w[0], w[1]).reshape(cy, cz, half)
     arrived(far_w, split, 11)
     others = pl.ds(partner * split, split)
-    w_ref[0, mine, :, lane_block(partner)] = far_u[:, :, lane_block(pole)] - my_mu * far_b[mine, :, lane_block(pole)]
-    w_ref[0, others, :, lane_block(partner)] = far_w[...] - my_mu * far_b[others, :, lane_block(pole)]
+    w_ref[mine, :, lane_block(partner)] = far_u[:, :, lane_block(pole)] - my_mu * far_b[mine, :, lane_block(pole)]
+    w_ref[others, :, lane_block(partner)] = far_w[...] - my_mu * far_b[others, :, lane_block(pole)]
 
     arrived(part2, fy - 1, 8)
     sum2[...] = jnp.sum(part2[...], axis=0)
@@ -257,8 +257,7 @@
     sent(far_w, split, 11)
 
     arrived(part2z, poles * fz - 1, 9)
-    total2 = jnp.sum(jnp.sum(part2z[...], axis=0), axis=1, keepdims=True)
-    w00, w01, w11, e00, e01, e11, c01, c10 = (total2[i : i + 1] for i in range(8))
+    w00, w01, w11, e00, e01, e11, c01, c10 = totals(part2z, all2, 8)
 
     def factors(mean, norm, ww, whw):
         nu = jnp.where(ww > 0.0, whw / jnp.where(ww > 0.0, ww, 1.0), mean)
@@ -269,26 +268,31 @@
         size = real * real + imag * imag
         return ((det - q * trace) * imag - real) / size, trace * imag / size
 
+    def gram(ref, upper, cross, lower):
+        lane = lax.broadcasted_iota(jnp.int32, (1, 128), 1)
+        ref[0:1, :] = jnp.where(lane == 0, upper, cross)[:, 0:2]
+        ref[1:2, :] = jnp.where(lane == 0, cross, lower)[:, 0:2]
+
     a0, f0 = factors(mu[0], m00, w00, e00)
     a1, f1 = factors(mu[1], m11, w11, e11)
-    coef_ref[0:1] = jnp.broadcast_to(jnp.where(first, a0, a1), (1, 128))
-    coef_ref[1:2] = jnp.broadcast_to(jnp.where(first, f0, f1), (1, 128))
-
-    corr_ref[0:1, 0:1] = a0 * a0 * m00 + f0 * f0 * w00
-    corr_ref[1:2, 1:2] = a1 * a1 * m11 + f1 * f1 * w11
+    a, f = jnp.where(first, a0, a1), jnp.where(first, f0, f1)
+    for block, base in ((lane_block(pole), own_b), (lane_block(partner), far_b)):
+        out_ref[0, :, :, block] = a * base[:, :, lane_block(pole)] + f * w_ref[:, :, block]
+
     cross = a0 * a1 * m01 + a0 * f1 * c01 + f0 * a1 * c10 + f0 * f1 * w01
-    corr_ref[0:1, 1:2] = cross
-    corr_ref[1:2, 0:1] = cross
-    energy_ref[0:1, 0:1] = a0 * a0 * mu[0] * m00 + 2.0 * a0 * f0 * w00 + f0 * f0 * e00
-    energy_ref[1:2, 1:2] = a1 * a1 * mu[1] * m11 + 2.0 * a1 * f1 * w11 + f1 * f1 * e11
+    gram(corr_ref, a0 * a0 * m00 + f0 * f0 * w00, cross, a1 * a1 * m11 + f1 * f1 * w11)
     cross = (
         a0 * a1 * (c01 + mu[1] * m01)
         + a0 * f1 * (w01 + mu[0] * c01)
         + f0 * a1 * (w01 + mu[1] * c10)
         + f0 * f1 * e01
     )
-    energy_ref[0:1, 1:2] = cross
-    energy_ref[1:2, 0:1] = cross
+    gram(
+        energy_ref,
+        a0 * a0 * mu[0] * m00 + 2.0 * a0 * f0 * w00 + f0 * f0 * e00,
+        cross,
+        a1 * a1 * mu[1] * m11 + 2.0 * a1 * f1 * w11 + f1 * f1 * e11,
+    )
     sent(part2z, poles * fz - 1, 9)
 
 
@@ -305,16 +309,15 @@
 
     x_block, y_block = vmem(cy, cz, nx), vmem(fy, cy, nx)
     sums = vmem(8, 128)
-    w, coef, corr, energy = pl.pallas_call(
+    filtered, corr, energy = pl.pallas_call(
         functools.partial(kernel, cy, cz, nx, fy, fz, poles),
         out_shape=(
             jax.ShapeDtypeStruct((1, cy, cz, nx), f32),
-            jax.ShapeDtypeStruct((8, 128), f32),
             jax.ShapeDtypeStruct((columns, columns), f32),
             jax.ShapeDtypeStruct((columns, columns), f32),
         ),
         in_specs=[in_hbm] * 5,
-        out_specs=(in_vmem,) * 4,
+        out_specs=(in_vmem,) * 3,
         scratch_shapes=[
             x_block, x_block, vmem(cy, cz, half),
             vmem(nx, nx), vmem(cy * fy, cy * fy), vmem(cz * fz, cz * fz),
@@ -322,26 +325,30 @@
             y_block, y_block, vmem(fz, cz, nx),
             y_block, vmem(fz, cz, nx), y_block, vmem(fz, cz, nx),
             y_block, y_block, vmem(fz, cz, nx),
-            vmem(cy // 2, cz, nx), vmem(cy // 2, cz, half),
-            sums, sums, sums, sums,
+            vmem(cy // 2, cz, nx), vmem(cy // 2, cz, half), x_block,
+            sums, sums, sums, sums, sums, sums,
             vmem(fy, 8, 128), vmem(fy, 8, 128), vmem(poles * fz, 8, 128), vmem(poles * fz, 8, 128),
             pltpu.SemaphoreType.DMA((8,)),
             pltpu.SemaphoreType.DMA((12,)),
             pltpu.SemaphoreType.DMA((12,)),
         ],
         compiler_params=pltpu.CompilerParams(
-            collective_id=0, has_side_effects=True, vmem_limit_bytes=62 * 1024 * 1024
+            collective_id=0, has_side_effects=True, vmem_limit_bytes=32 * 1024 * 1024
         ),
     )(
-        states,
-        potential,
-        jnp.asarray(axis_operator(nx)),
-        jnp.asarray(axis_operator(cy * fy)),
-        jnp.asarray(axis_operator(cz * fz)),
+        *(
+            pltpu.with_memory_space_constraint(operand, pltpu.HBM)
+            for operand in (
+                states,
+                potential,
+                jnp.asarray(axis_operator(nx)),
+                jnp.asarray(axis_operator(cy * fy)),
+                jnp.asarray(axis_operator(cz * fz)),
+            )
+        )
     )
-    mine = lax.dynamic_slice_in_dim(states, lax.axis_index("pole"), 1, 0)
     cells = 1.0 / float(nx * cy * fy * cz * fz)
-    return coef[0, 0] * mine + coef[1, 0] * w, corr * cells, energy * cells
+    return filtered, corr * cells, energy * cells
 
 
 def solution(mesh):

time: 46.6 us -> 41.4 us (0.89)
  other arithmetic: 3.44 us -> 0.57 us
  Pallas kernels: 41.1 us -> 39.4 us
  local copies, waits for them, and re-layouts: 1.28 us -> 0.65 us
    add x1 -> x0, other arithmetic: 2.87 us -> none  [local(): return (coef[0, 0] * mine + coef[1, 0] * w, corr * cells, energy * cells)]
    pallas_call x1, Pallas kernels: 41.1 us -> 39.4 us  [local(): pl.pallas_call(functools.partial(kernel, cy, cz, nx, fy, fz, poles), out_...]
    slice x1 -> x0, local copies, waits for them, and re-layouts: 1.27 us -> none  [local(): return (coef[0, 0] * mine + coef[1, 0] * w, corr * cells, energy * cells)]
    unnamed x6 -> x1, local copies, waits for them, and re-layouts: 0.01 us -> 0.65 us
where the time goes in v3:
time: 41.4 us; the launch traced here: 41.3 us
  Pallas kernels  39.4 us (95%)
  local copies, waits for them, and re-layouts  0.65 us (2%)
  between operations  0.64 us (2%)
  other arithmetic  0.57 us (1%)
    pallas_call x1, Pallas kernels, local(): pl.pallas_call(functools.partial(kernel, cy, cz, nx, fy, fz, poles), out_...  39.4 us

profile of v3, /device:TPU:1, one launch (start us, length us, event | category | flops | bytes accessed | tf_op | source)
XLA Modules:
  0.0 41.3 jit_solution(8939250960917330789)
XLA Ops:
  0.6 39.4 %shard_map.76 = (f32[1,16,8,256]{3,2,1,0:T(8,128)S(1)}, f32[2,2]{1,0:T(2,128)S(1)}, f32[2,2]{1,0:T(2,128)S(1)}) custom-call(f32[2,16,8,256]{3,2,1,0:T(8,128)} %states_hbm.1, f32[16,8,256]{2,1,0:T(8,128)} %pot_hbm.1, f32[256,256]{1,0:T(8,128)} %constant.6.clone.dx_hbm, f32[128,128]{1,0:T(8,128)} %constant.7.clone.dy_hbm.dz_hbm, ...), custom_call_target="tpu_custom_call" | custom-call | tf_op jit(solution)/shard_map/pallas_call | solution.py:312
  40.1 0.6 %broadcast_multiply_fusion = (f32[2,2]{1,0:T(2,128)}, f32[2,2]{1,0:T(2,128)}) fusion(f32[2,2]{1,0:T(2,128)S(1)} %get-tuple-element.8, f32[2,2]{1,0:T(2,128)S(1)} %get-tuple-element.7), kind=kLoop, calls=%fused_computation | loop fusion | flops 8 | bytes 64 | tf_op jit(solution)/shard_map/mul | solution.py:351
  40.7 0.7 %copy.9 = f32[1,16,8,256]{3,2,1,0:T(8,128)} copy(f32[1,16,8,256]{3,2,1,0:T(8,128)S(1)} %get-tuple-element.14) | data formatting | bytes 262144

commit v4 on v3

--- a/solution.py
+++ b/solution.py
@@ -38,8 +38,8 @@
     states_hbm, pot_hbm, dx_hbm, dy_hbm, dz_hbm,
     out_ref, corr_ref, energy_ref,
     own_b, far_b, v_ref, dx_ref, dy_ref, dz_ref, s_ref, u_ref,
-    ysend, yb, zb, ymul, zmul, yback, zback, yusend, yu, zu, far_u, far_w, w_ref,
-    acc1, acc2, sum1, sum2, all1, all2, part1, part2, part1z, part2z,
+    ysend, yb, zb, ymul, zmul, yback, zback, yusend, yu, zu, far_u, far_w, u_far, whole_u,
+    acc, sum_y, part_y, part_z, all_sums, lane_sums, cancelled,
     load_sem, send_sem, recv_sem,
 ):
     pole, my, mz = lax.axis_index("pole"), lax.axis_index("fy"), lax.axis_index("fz")
@@ -104,11 +104,6 @@
     def sent(dst, count, slot):
         whole = dst.at[pl.ds(0, count)]
         pltpu.make_async_copy(whole, whole, send_sem.at[slot]).wait()
-
-    def totals(parts, buffer, count):
-        whole = jnp.sum(jnp.sum(parts[...], axis=0), axis=1, keepdims=True)
-        buffer[...] = jnp.broadcast_to(whole, (8, 128))
-        return [buffer[i : i + 1] for i in range(count)]
 
     barrier = pltpu.get_barrier_semaphore()
 
@@ -154,11 +149,10 @@
         whole = jnp.concatenate([b[c], column(far_b, c)], axis=1)
         s.append(v * b[c] + dot(whole, dx_ref[:, col0]))
         s_ref[:, :, c * half : (c + 1) * half] = s[c].reshape(cy, cz, half)
-    acc1[0:1] = lanes(b[0] * b[0])
-    acc1[1:2] = lanes(b[0] * b[1])
-    acc1[2:3] = lanes(b[1] * b[1])
-    acc1[5:8] = jnp.zeros((3, 128), jnp.float32)
-    own = [lanes(b[c] * s[c]) for c in range(2)]
+    acc[0:1] = lanes(b[0] * b[0])
+    acc[1:2] = lanes(b[0] * b[1])
+    acc[2:3] = lanes(b[1] * b[1])
+    acc[12:16] = jnp.zeros((4, 128), jnp.float32)
 
     arrived(zb, fz - 1, 1)
     zmul[...] = dot(dz_ref[...], flat(zb)).reshape(fz, cz, nx)
@@ -171,78 +165,62 @@
         push_y(ymul, yback, step, 2)
     yback[my] = ymul[my]
 
-    both = lanes(flat(zb) * flat(zmul)) + lanes(flat(yb) * flat(ymul))
-    acc1[3:4] = own[0] + both[:, col0]
-    acc1[4:5] = own[1] + both[:, col1]
-    spread(acc1, part1, fy, my, at_y, 6)
-
     arrived(zback, fz - 1, 3)
     s_ref[...] += zback[...]
     arrived(yback, fy - 1, 2)
     u_ref[...] = s_ref[...] + jnp.swapaxes(yback[...], 0, 1)
     yusend[...] = jnp.swapaxes(u_ref[...], 0, 1)
-    push(u_ref.at[pl.ds(partner * split, split)], far_u, across, 10)
+    push(u_ref.at[pl.ds(partner * split, split)], far_u, across, 6)
     exchange(yusend, yu, 4, u_ref, zu, 5)
-    arrived(part1, fy - 1, 6)
-    sum1[...] = jnp.sum(part1[...], axis=0)
-    spread(sum1, part1z, poles * fz, plane, at_plane, 7)
-    push(u_ref.at[pl.ds(pole * split, split), :, lane_block(partner)], far_w, across, 11)
-
-    arrived(part1z, poles * fz - 1, 7)
-    m00, m01, m11, h00, h11 = totals(part1z, all1, 5)
-    mu = [h00 / m00, h11 / m11]
-
-    w = [column(u_ref, c) - mu[c] * b[c] for c in range(2)]
-    acc2[0:1] = lanes(w[0] * w[0])
-    acc2[1:2] = lanes(w[0] * w[1])
-    acc2[2:3] = lanes(w[1] * w[1])
-    acc2[6:7] = lanes(b[0] * w[1])
-    acc2[7:8] = lanes(b[1] * w[0])
-    applied = [v * w[0], v * w[1]]
-    terms = [lanes(w[0] * applied[0]), lanes(w[0] * applied[1]), lanes(w[1] * applied[1])]
+    push(u_ref.at[pl.ds(pole * split, split), :, lane_block(partner)], far_w, across, 7)
+
+    u = [column(u_ref, c) for c in range(2)]
+    acc[3:4] = lanes(b[0] * u[0])
+    acc[4:5] = lanes(b[0] * u[1])
+    acc[5:6] = lanes(b[1] * u[1])
+    acc[6:7] = lanes(u[0] * u[0])
+    acc[7:8] = lanes(u[0] * u[1])
+    acc[8:9] = lanes(u[1] * u[1])
+    applied = [v * u[0], v * u[1]]
+    terms = [lanes(u[0] * applied[0]), lanes(u[0] * applied[1]), lanes(u[1] * applied[1])]
 
     def quadratic(left, right):
         terms[0] += lanes(left[0] * right[0])
         terms[1] += lanes(left[0] * right[1])
         terms[2] += lanes(left[1] * right[1])
 
-    arrived(far_u, split, 10)
-    mine = pl.ds(pole * split, split)
-    whole = []
+    arrived(far_u, split, 6)
+    mine, others = pl.ds(pole * split, split), pl.ds(partner * split, split)
     for c in range(2):
         block = slice(c * half, (c + 1) * half)
-        near_part = u_ref[mine, :, block] - mu[c] * own_b[mine, :, block]
-        far_part = far_u[:, :, block] - mu[c] * far_b[mine, :, block]
-        whole.append(jnp.concatenate([near_part, far_part], axis=2).reshape(split * cz, nx))
+        whole_u[c] = jnp.concatenate([u_ref[mine, :, block], far_u[:, :, block]], axis=2).reshape(split * cz, nx)
+    whole = [whole_u[0], whole_u[1]]
     product = [dot(whole[c], dx_ref[...]) for c in range(2)]
-    x_terms = [lanes(whole[0] * product[0]), lanes(whole[0] * product[1]), lanes(whole[1] * product[1])]
+    for part in (col0, col1):
+        quadratic([left[:, part] for left in whole], [right[:, part] for right in product])
+
+    def pencil(operator, u_pencil):
+        product = dot(operator[...], flat(u_pencil))
+        left = flat(u_pencil)
+        quadratic([left[:, col0], left[:, col1]], [product[:, col0], product[:, col1]])
+
+    arrived(zu, fz - 1, 5)
+    pencil(dz_ref, zu)
+    arrived(yu, fy - 1, 4)
+    pencil(dy_ref, yu)
     for i in range(3):
-        terms[i] = terms[i] + x_terms[i][:, col0] + x_terms[i][:, col1]
-
-    def pencil(operator, u_pencil, b_pencil):
-        left = [column(u_pencil, c) - mu[c] * column(b_pencil, c) for c in range(2)]
-        quadratic(left, [dot(operator[...], left[c]) for c in range(2)])
-
-    arrived(zu, fz - 1, 5)
-    pencil(dz_ref, zu, zb)
-    arrived(yu, fy - 1, 4)
-    pencil(dy_ref, yu, yb)
-    for i in range(3):
-        acc2[3 + i : 4 + i] = terms[i]
-
-    spread(acc2, part2, fy, my, at_y, 8)
+        acc[9 + i : 10 + i] = terms[i]
+
+    spread(acc, part_y, fy, my, at_y, 8)
 
     first = pole == 0
-    my_mu = jnp.where(first, mu[0], mu[1])
-    w_ref[:, :, lane_block(pole)] = jnp.where(first, w[0], w[1]).reshape(cy, cz, half)
-    arrived(far_w, split, 11)
-    others = pl.ds(partner * split, split)
-    w_ref[mine, :, lane_block(partner)] = far_u[:, :, lane_block(pole)] - my_mu * far_b[mine, :, lane_block(pole)]
-    w_ref[others, :, lane_block(partner)] = far_w[...] - my_mu * far_b[others, :, lane_block(pole)]
-
-    arrived(part2, fy - 1, 8)
-    sum2[...] = jnp.sum(part2[...], axis=0)
-    spread(sum2, part2z, poles * fz, plane, at_plane, 9)
+    arrived(far_w, split, 7)
+    u_far[mine] = far_u[:, :, lane_block(pole)]
+    u_far[others] = far_w[...]
+
+    arrived(part_y, fy - 1, 8)
+    sum_y[...] = jnp.sum(part_y[...], axis=0)
+    spread(sum_y, part_z, poles * fz, plane, at_plane, 9)
 
     sent(yb, fy - 1, 0)
     sent(zb, fz - 1, 1)
@@ -250,18 +228,36 @@
     sent(zback, fz - 1, 3)
     sent(yu, fy - 1, 4)
     sent(zu, fz - 1, 5)
-    sent(part1, fy - 1, 6)
-    sent(part1z, poles * fz - 1, 7)
-    sent(part2, fy - 1, 8)
-    sent(far_u, split, 10)
-    sent(far_w, split, 11)
-
-    arrived(part2z, poles * fz - 1, 9)
-    w00, w01, w11, e00, e01, e11, c01, c10 = totals(part2z, all2, 8)
+    sent(far_u, split, 6)
+    sent(far_w, split, 7)
+    sent(part_y, fy - 1, 8)
+
+    arrived(part_z, poles * fz - 1, 9)
+    by_lane = jnp.sum(part_z[...], axis=0)
+
+    def totals(value, buffer):
+        buffer[...] = jnp.broadcast_to(jnp.sum(value, axis=1, keepdims=True), value.shape)
+        return [buffer[i : i + 1] for i in range(value.shape[0])]
+
+    m00, m01, m11, h00, _, h11 = totals(by_lane, all_sums)[:6]
+    mu = [h00 / m00, h11 / m11]
+    lane_sums[...] = by_lane
+    l00, l01, l11, b00, b01, b11, u00, u01, u11, e00, e01, e11 = (lane_sums[i : i + 1] for i in range(12))
+    cancelled[0:1] = u00 - mu[0] * (2.0 * b00 - mu[0] * l00)
+    cancelled[1:2] = u01 - (mu[0] + mu[1]) * b01 + mu[0] * mu[1] * l01
+    cancelled[2:3] = u11 - mu[1] * (2.0 * b11 - mu[1] * l11)
+    cancelled[3:4] = e00 - mu[0] * (2.0 * u00 - mu[0] * b00)
+    cancelled[4:5] = e01 - (mu[0] + mu[1]) * u01 + mu[0] * mu[1] * b01
+    cancelled[5:6] = e11 - mu[1] * (2.0 * u11 - mu[1] * b11)
+    cancelled[6:7] = b01 - mu[1] * l01
+    cancelled[7:8] = b01 - mu[0] * l01
+    w00, w01, w11, e00, e01, e11, c01, c10 = totals(cancelled[...], cancelled)
+
+    top = 1.5 * math.pi**2 + 3.0
 
     def factors(mean, norm, ww, whw):
-        nu = jnp.where(ww > 0.0, whw / jnp.where(ww > 0.0, ww, 1.0), mean)
-        t2 = ww / norm
+        nu = jnp.where(ww > 0.0, jnp.clip(whw / jnp.where(ww > 0.0, ww, 1.0), 0.0, top), mean)
+        t2 = jnp.maximum(ww, 0.0) / norm
         p, q = mean - 1.0, nu - 1.0
         trace, det = p + q, p * q - t2
         real, imag = det * det - 1.0, 2.0 * det - trace * trace
@@ -276,9 +272,13 @@
     a0, f0 = factors(mu[0], m00, w00, e00)
     a1, f1 = factors(mu[1], m11, w11, e11)
     a, f = jnp.where(first, a0, a1), jnp.where(first, f0, f1)
-    for block, base in ((lane_block(pole), own_b), (lane_block(partner), far_b)):
-        out_ref[0, :, :, block] = a * base[:, :, lane_block(pole)] + f * w_ref[:, :, block]
-
+    my_mu = jnp.where(first, mu[0], mu[1])
+    column_block = lane_block(pole)
+    for block, base, applied in (
+        (lane_block(pole), own_b[:, :, column_block], u_ref[:, :, column_block]),
+        (lane_block(partner), far_b[:, :, column_block], u_far[...]),
+    ):
+        out_ref[0, :, :, block] = a * base + f * (applied - my_mu * base)
     cross = a0 * a1 * m01 + a0 * f1 * c01 + f0 * a1 * c10 + f0 * f1 * w01
     gram(corr_ref, a0 * a0 * m00 + f0 * f0 * w00, cross, a1 * a1 * m11 + f1 * f1 * w11)
     cross = (
@@ -293,7 +293,7 @@
         cross,
         a1 * a1 * mu[1] * m11 + 2.0 * a1 * f1 * w11 + f1 * f1 * e11,
     )
-    sent(part2z, poles * fz - 1, 9)
+    sent(part_z, poles * fz - 1, 9)
 
 
 def local(states, potential):
@@ -308,7 +308,7 @@
         return pltpu.VMEM(shape, f32)
 
     x_block, y_block = vmem(cy, cz, nx), vmem(fy, cy, nx)
-    sums = vmem(8, 128)
+    sums = vmem(16, 128)
     filtered, corr, energy = pl.pallas_call(
         functools.partial(kernel, cy, cz, nx, fy, fz, poles),
         out_shape=(
@@ -325,12 +325,11 @@
             y_block, y_block, vmem(fz, cz, nx),
             y_block, vmem(fz, cz, nx), y_block, vmem(fz, cz, nx),
             y_block, y_block, vmem(fz, cz, nx),
-            vmem(cy // 2, cz, nx), vmem(cy // 2, cz, half), x_block,
-            sums, sums, sums, sums, sums, sums,
-            vmem(fy, 8, 128), vmem(fy, 8, 128), vmem(poles * fz, 8, 128), vmem(poles * fz, 8, 128),
+            vmem(cy // 2, cz, nx), vmem(cy // 2, cz, half), vmem(cy, cz, half), vmem(columns, cy // 2 * cz, nx),
+            sums, sums, vmem(fy, 16, 128), vmem(poles * fz, 16, 128), sums, sums, vmem(8, 128),
             pltpu.SemaphoreType.DMA((8,)),
-            pltpu.SemaphoreType.DMA((12,)),
-            pltpu.SemaphoreType.DMA((12,)),
+            pltpu.SemaphoreType.DMA((10,)),
+            pltpu.SemaphoreType.DMA((10,)),
         ],
         compiler_params=pltpu.CompilerParams(
             collective_id=0, has_side_effects=True, vmem_limit_bytes=32 * 1024 * 1024

time: 41.4 us -> 39.2 us (0.947)
  Pallas kernels: 39.4 us -> 37.3 us
    pallas_call x1, Pallas kernels: 39.4 us -> 37.3 us  [local(): pl.pallas_call(functools.partial(kernel, cy, cz, nx, fy, fz, poles), out_...]
where the time goes in v4:
time: 39.2 us; the launch traced here: 39.1 us
  Pallas kernels  37.3 us (95%)
  local copies, waits for them, and re-layouts  0.65 us (2%)
  between operations  0.64 us (2%)
  other arithmetic  0.57 us (1%)
    pallas_call x1, Pallas kernels, local(): pl.pallas_call(functools.partial(kernel, cy, cz, nx, fy, fz, poles), out_...  37.3 us

profile of v4, /device:TPU:1, one launch (start us, length us, event | category | flops | bytes accessed | tf_op | source)
XLA Modules:
  0.0 39.1 jit_solution(357216038038670929)
XLA Ops:
  0.6 37.3 %shard_map.76 = (f32[1,16,8,256]{3,2,1,0:T(8,128)S(1)}, f32[2,2]{1,0:T(2,128)S(1)}, f32[2,2]{1,0:T(2,128)S(1)}) custom-call(f32[2,16,8,256]{3,2,1,0:T(8,128)} %states_hbm.1, f32[16,8,256]{2,1,0:T(8,128)} %pot_hbm.1, f32[256,256]{1,0:T(8,128)} %constant.6.clone.dx_hbm, f32[128,128]{1,0:T(8,128)} %constant.7.clone.dy_hbm.dz_hbm, ...), custom_call_target="tpu_custom_call" | custom-call | tf_op jit(solution)/shard_map/pallas_call | solution.py:312
  37.9 0.6 %broadcast_multiply_fusion = (f32[2,2]{1,0:T(2,128)}, f32[2,2]{1,0:T(2,128)}) fusion(f32[2,2]{1,0:T(2,128)S(1)} %get-tuple-element.8, f32[2,2]{1,0:T(2,128)S(1)} %get-tuple-element.7), kind=kLoop, calls=%fused_computation | loop fusion | flops 8 | bytes 64 | tf_op jit(solution)/shard_map/mul | solution.py:350
  38.5 0.7 %copy.9 = f32[1,16,8,256]{3,2,1,0:T(8,128)} copy(f32[1,16,8,256]{3,2,1,0:T(8,128)S(1)} %get-tuple-element.14) | data formatting | bytes 262144

commit v5 on v4

--- a/solution.py
+++ b/solution.py
@@ -39,7 +39,7 @@
     out_ref, corr_ref, energy_ref,
     own_b, far_b, v_ref, dx_ref, dy_ref, dz_ref, s_ref, u_ref,
     ysend, yb, zb, ymul, zmul, yback, zback, yusend, yu, zu, far_u, far_w, u_far, whole_u,
-    acc, sum_y, part_y, part_z, all_sums, lane_sums, cancelled,
+    acc, mine_sums, core_sums, chip_sums, parts, rows_ref,
     load_sem, send_sem, recv_sem,
 ):
     pole, my, mz = lax.axis_index("pole"), lax.axis_index("fy"), lax.axis_index("fz")
@@ -79,23 +79,15 @@
     def push_z(src, dst, step, slot):
         push(src.at[lax.rem(mz + step, fz)], dst.at[mz], at_z(step), slot)
 
-    def exchange(ysrc, ydst, yslot, zsrc, zdst, zslot):
-        ysteps, zsteps = far_first(fy), far_first(fz)
-        for i in range(max(fy, fz) - 1):
-            if i < len(ysteps):
-                push_y(ysrc, ydst, ysteps[i], yslot)
-            if i < len(zsteps):
-                push_z(zsrc, zdst, zsteps[i], zslot)
-        ydst[my] = ysrc[my]
-        zdst[mz] = zsrc[mz]
-
-    def spread(src, dst, count, me, place, slot):
-        def body(step, carry):
-            push(src, dst.at[me], place(step), slot)
-            return carry
-
-        lax.fori_loop(1, count, body, 0)
-        dst[me] = src[...]
+    def scatter_y(src, dst, slot):
+        for step in far_first(fy):
+            push_y(src, dst, step, slot)
+        dst[my] = src[my]
+
+    def scatter_z(src, dst, slot):
+        for step in far_first(fz):
+            push_z(src, dst, step, slot)
+        dst[mz] = src[mz]
 
     def arrived(dst, count, slot):
         whole = dst.at[pl.ds(0, count)]
@@ -132,7 +124,8 @@
     ysend[...] = jnp.swapaxes(own_b[...], 0, 1)
     pl.semaphore_wait(barrier, fy + fz - 1)
 
-    exchange(ysend, yb, 0, own_b, zb, 1)
+    scatter_y(ysend, yb, 0)
+    scatter_z(own_b, zb, 1)
     for copy in rest:
         copy.wait()
 
@@ -156,22 +149,19 @@
 
     arrived(zb, fz - 1, 1)
     zmul[...] = dot(dz_ref[...], flat(zb)).reshape(fz, cz, nx)
-    for step in far_first(fz):
-        push_z(zmul, zback, step, 3)
-    zback[mz] = zmul[mz]
+    scatter_z(zmul, zback, 3)
     arrived(yb, fy - 1, 0)
     ymul[...] = dot(dy_ref[...], flat(yb)).reshape(fy, cy, nx)
-    for step in far_first(fy):
-        push_y(ymul, yback, step, 2)
-    yback[my] = ymul[my]
+    scatter_y(ymul, yback, 2)
 
     arrived(zback, fz - 1, 3)
-    s_ref[...] += zback[...]
+    yusend[...] = jnp.swapaxes(s_ref[...] + zback[...], 0, 1)
     arrived(yback, fy - 1, 2)
-    u_ref[...] = s_ref[...] + jnp.swapaxes(yback[...], 0, 1)
-    yusend[...] = jnp.swapaxes(u_ref[...], 0, 1)
+    yusend[...] += yback[...]
+    scatter_y(yusend, yu, 4)
+    u_ref[...] = jnp.swapaxes(yusend[...], 0, 1)
     push(u_ref.at[pl.ds(partner * split, split)], far_u, across, 6)
-    exchange(yusend, yu, 4, u_ref, zu, 5)
+    scatter_z(u_ref, zu, 5)
     push(u_ref.at[pl.ds(pole * split, split), :, lane_block(partner)], far_w, across, 7)
 
     u = [column(u_ref, c) for c in range(2)]
@@ -211,16 +201,34 @@
     for i in range(3):
         acc[9 + i : 10 + i] = terms[i]
 
-    spread(acc, part_y, fy, my, at_y, 8)
+    lane = lax.broadcasted_iota(jnp.int32, (16, 128), 1)
+    row = lax.broadcasted_iota(jnp.int32, (16, 128), 0)
+    folded = acc[...]
+    for shift in (64, 32, 16, 8):
+        folded = folded + pltpu.roll(folded, shift, 1)
+    mine_sums[...] = jnp.sum(jnp.where(lane // 8 == row, folded, 0.0), axis=0, keepdims=True)
+    push(mine_sums, core_sums, (pole, my, mz + 1 - 2 * lax.rem(mz, 2)), 8)
 
     first = pole == 0
     arrived(far_w, split, 7)
     u_far[mine] = far_u[:, :, lane_block(pole)]
     u_far[others] = far_w[...]
 
-    arrived(part_y, fy - 1, 8)
-    sum_y[...] = jnp.sum(part_y[...], axis=0)
-    spread(sum_y, part_z, poles * fz, plane, at_plane, 9)
+    whole_core = core_sums.at[pl.ds(0, 1)]
+    pltpu.make_async_copy(whole_core, whole_core, recv_sem.at[8]).wait()
+    chips = poles * fz // 2
+    chip = my * chips + plane // 2
+    chip_sums[...] = mine_sums[...] + core_sums[...]
+    for step_y in far_first(fy) + [0]:
+
+        def body(step, carry, step_y=step_y):
+            other = lax.rem(plane + 2 * step, 2 * chips)
+            place = (other // fz, lax.rem(my + step_y, fy), lax.rem(other, fz))
+            push(chip_sums, parts.at[chip], place, 9)
+            return carry
+
+        lax.fori_loop(0 if step_y else 1, chips, body, 0)
+    parts[chip] = chip_sums[...]
 
     sent(yb, fy - 1, 0)
     sent(zb, fz - 1, 1)
@@ -230,28 +238,36 @@
     sent(zu, fz - 1, 5)
     sent(far_u, split, 6)
     sent(far_w, split, 7)
-    sent(part_y, fy - 1, 8)
-
-    arrived(part_z, poles * fz - 1, 9)
-    by_lane = jnp.sum(part_z[...], axis=0)
-
-    def totals(value, buffer):
-        buffer[...] = jnp.broadcast_to(jnp.sum(value, axis=1, keepdims=True), value.shape)
-        return [buffer[i : i + 1] for i in range(value.shape[0])]
-
-    m00, m01, m11, h00, _, h11 = totals(by_lane, all_sums)[:6]
+    pltpu.make_async_copy(whole_core, whole_core, send_sem.at[8]).wait()
+
+    arrived(parts, fy * chips - 1, 9)
+    total = jnp.sum(parts[...], axis=0)
+    slim = lax.broadcasted_iota(jnp.int32, (8, 128), 1) < 8
+
+    def totals(values):
+        for i, value in enumerate(values):
+            rows_ref[i : i + 1] = value
+        summed = jnp.sum(jnp.where(slim, rows_ref[...], 0.0), axis=1, keepdims=True)
+        rows_ref[...] = jnp.broadcast_to(summed, (8, 128))
+        return [rows_ref[i : i + 1] for i in range(len(values))]
+
+    l00, l01, l11, b00, b01, b11, u00, u01, u11, e00, e01, e11 = (
+        pltpu.roll(total, (128 - 8 * i) % 128, 1) if i else total for i in range(12)
+    )
+    m00, m01, m11, h00, h11 = totals([l00, l01, l11, b00, b11])
     mu = [h00 / m00, h11 / m11]
-    lane_sums[...] = by_lane
-    l00, l01, l11, b00, b01, b11, u00, u01, u11, e00, e01, e11 = (lane_sums[i : i + 1] for i in range(12))
-    cancelled[0:1] = u00 - mu[0] * (2.0 * b00 - mu[0] * l00)
-    cancelled[1:2] = u01 - (mu[0] + mu[1]) * b01 + mu[0] * mu[1] * l01
-    cancelled[2:3] = u11 - mu[1] * (2.0 * b11 - mu[1] * l11)
-    cancelled[3:4] = e00 - mu[0] * (2.0 * u00 - mu[0] * b00)
-    cancelled[4:5] = e01 - (mu[0] + mu[1]) * u01 + mu[0] * mu[1] * b01
-    cancelled[5:6] = e11 - mu[1] * (2.0 * u11 - mu[1] * b11)
-    cancelled[6:7] = b01 - mu[1] * l01
-    cancelled[7:8] = b01 - mu[0] * l01
-    w00, w01, w11, e00, e01, e11, c01, c10 = totals(cancelled[...], cancelled)
+    w00, w01, w11, e00, e01, e11, c01, c10 = totals(
+        [
+            u00 - mu[0] * (2.0 * b00 - mu[0] * l00),
+            u01 - (mu[0] + mu[1]) * b01 + mu[0] * mu[1] * l01,
+            u11 - mu[1] * (2.0 * b11 - mu[1] * l11),
+            e00 - mu[0] * (2.0 * u00 - mu[0] * b00),
+            e01 - (mu[0] + mu[1]) * u01 + mu[0] * mu[1] * b01,
+            e11 - mu[1] * (2.0 * u11 - mu[1] * b11),
+            b01 - mu[1] * l01,
+            b01 - mu[0] * l01,
+        ]
+    )
 
     top = 1.5 * math.pi**2 + 3.0
 
@@ -293,7 +309,7 @@
         cross,
         a1 * a1 * mu[1] * m11 + 2.0 * a1 * f1 * w11 + f1 * f1 * e11,
     )
-    sent(part_z, poles * fz - 1, 9)
+    sent(parts, fy * chips - 1, 9)
 
 
 def local(states, potential):
@@ -308,7 +324,6 @@
         return pltpu.VMEM(shape, f32)
 
     x_block, y_block = vmem(cy, cz, nx), vmem(fy, cy, nx)
-    sums = vmem(16, 128)
     filtered, corr, energy = pl.pallas_call(
         functools.partial(kernel, cy, cz, nx, fy, fz, poles),
         out_shape=(
@@ -326,7 +341,7 @@
             y_block, vmem(fz, cz, nx), y_block, vmem(fz, cz, nx),
             y_block, y_block, vmem(fz, cz, nx),
             vmem(cy // 2, cz, nx), vmem(cy // 2, cz, half), vmem(cy, cz, half), vmem(columns, cy // 2 * cz, nx),
-            sums, sums, vmem(fy, 16, 128), vmem(poles * fz, 16, 128), sums, sums, vmem(8, 128),
+            vmem(16, 128), vmem(1, 128), vmem(1, 128), vmem(1, 128), vmem(fy * poles * fz // 2, 1, 128), vmem(8, 128),
             pltpu.SemaphoreType.DMA((8,)),
             pltpu.SemaphoreType.DMA((10,)),
             pltpu.SemaphoreType.DMA((10,)),

time: 39.2 us -> 37.3 us (0.952)
  Pallas kernels: 37.3 us -> 35.4 us
    pallas_call x1, Pallas kernels: 37.3 us -> 35.4 us  [local(): pl.pallas_call(functools.partial(kernel, cy, cz, nx, fy, fz, poles), out_...]
where the time goes in v5:
time: 37.3 us; the launch traced here: 37.2 us
  Pallas kernels  35.4 us (95%)
  local copies, waits for them, and re-layouts  0.65 us (2%)
  between operations  0.64 us (2%)
  other arithmetic  0.57 us (2%)
    pallas_call x1, Pallas kernels, local(): pl.pallas_call(functools.partial(kernel, cy, cz, nx, fy, fz, poles), out_...  35.4 us

profile of v5, /device:TPU:1, one launch (start us, length us, event | category | flops | bytes accessed | tf_op | source)
XLA Modules:
  0.0 37.2 jit_solution(11743637288405668559)
XLA Ops:
  0.6 35.4 %shard_map.76 = (f32[1,16,8,256]{3,2,1,0:T(8,128)S(1)}, f32[2,2]{1,0:T(2,128)S(1)}, f32[2,2]{1,0:T(2,128)S(1)}) custom-call(f32[2,16,8,256]{3,2,1,0:T(8,128)} %states_hbm.1, f32[16,8,256]{2,1,0:T(8,128)} %pot_hbm.1, f32[256,256]{1,0:T(8,128)} %constant.6.clone.dx_hbm, f32[128,128]{1,0:T(8,128)} %constant.7.clone.dy_hbm.dz_hbm, ...), custom_call_target="tpu_custom_call" | custom-call | tf_op jit(solution)/shard_map/pallas_call | solution.py:327
  36.0 0.6 %broadcast_multiply_fusion = (f32[2,2]{1,0:T(2,128)}, f32[2,2]{1,0:T(2,128)}) fusion(f32[2,2]{1,0:T(2,128)S(1)} %get-tuple-element.8, f32[2,2]{1,0:T(2,128)S(1)} %get-tuple-element.7), kind=kLoop, calls=%fused_computation | loop fusion | flops 8 | bytes 64 | tf_op jit(solution)/shard_map/mul | solution.py:365
  36.6 0.7 %copy.9 = f32[1,16,8,256]{3,2,1,0:T(8,128)} copy(f32[1,16,8,256]{3,2,1,0:T(8,128)S(1)} %get-tuple-element.14) | data formatting | bytes 262144

commit v6 on v5

--- a/solution.py
+++ b/solution.py
@@ -38,7 +38,7 @@
     states_hbm, pot_hbm, dx_hbm, dy_hbm, dz_hbm,
     out_ref, corr_ref, energy_ref,
     own_b, far_b, v_ref, dx_ref, dy_ref, dz_ref, s_ref, u_ref,
-    ysend, yb, zb, ymul, zmul, yback, zback, yusend, yu, zu, far_u, far_w, u_far, whole_u,
+    ysend, yb, zb, ymul, zmul, yback, zback, yusend, yu, zu, far_u, far_w, u_far, xmul,
     acc, mine_sums, core_sums, chip_sums, parts, rows_ref,
     load_sem, send_sem, recv_sem,
 ):
@@ -155,13 +155,13 @@
     scatter_y(ymul, yback, 2)
 
     arrived(zback, fz - 1, 3)
-    yusend[...] = jnp.swapaxes(s_ref[...] + zback[...], 0, 1)
+    s_ref[...] += zback[...]
+    yusend[...] = jnp.swapaxes(s_ref[...], 0, 1)
+    scatter_y(yusend, yu, 4)
     arrived(yback, fy - 1, 2)
-    yusend[...] += yback[...]
-    scatter_y(yusend, yu, 4)
-    u_ref[...] = jnp.swapaxes(yusend[...], 0, 1)
+    u_ref[...] = s_ref[...] + jnp.swapaxes(yback[...], 0, 1)
+    scatter_z(u_ref, zu, 5)
     push(u_ref.at[pl.ds(partner * split, split)], far_u, across, 6)
-    scatter_z(u_ref, zu, 5)
     push(u_ref.at[pl.ds(pole * split, split), :, lane_block(partner)], far_w, across, 7)
 
     u = [column(u_ref, c) for c in range(2)]
@@ -179,25 +179,25 @@
         terms[1] += lanes(left[0] * right[1])
         terms[2] += lanes(left[1] * right[1])
 
+    for c in range(2):
+        xmul[:, :, c * nx : (c + 1) * nx] = dot(u[c], dx_ref[0:half, :]).reshape(cy, cz, 2 * half)
+    quadratic(u, [xmul[:, :, c * nx : c * nx + half].reshape(rows, half) for c in range(2)])
+    mine, others = pl.ds(pole * split, split), pl.ds(partner * split, split)
+    between = [xmul[mine, :, c * nx + half : (c + 1) * nx].reshape(-1, half) for c in range(2)]
+
+    def pencil(operator, left):
+        product = dot(operator[...], left)
+        quadratic([left[:, col0], left[:, col1]], [product[:, col0], product[:, col1]])
+
+    arrived(yu, fy - 1, 4)
+    pencil(dy_ref, flat(yu) + flat(ymul))
     arrived(far_u, split, 6)
-    mine, others = pl.ds(pole * split, split), pl.ds(partner * split, split)
-    for c in range(2):
-        block = slice(c * half, (c + 1) * half)
-        whole_u[c] = jnp.concatenate([u_ref[mine, :, block], far_u[:, :, block]], axis=2).reshape(split * cz, nx)
-    whole = [whole_u[0], whole_u[1]]
-    product = [dot(whole[c], dx_ref[...]) for c in range(2)]
-    for part in (col0, col1):
-        quadratic([left[:, part] for left in whole], [right[:, part] for right in product])
-
-    def pencil(operator, u_pencil):
-        product = dot(operator[...], flat(u_pencil))
-        left = flat(u_pencil)
-        quadratic([left[:, col0], left[:, col1]], [product[:, col0], product[:, col1]])
-
+    far = [column(far_u, c) for c in range(2)]
+    terms[0] += 2.0 * lanes(far[0] * between[0])
+    terms[1] += lanes(far[0] * between[1] + far[1] * between[0])
+    terms[2] += 2.0 * lanes(far[1] * between[1])
     arrived(zu, fz - 1, 5)
-    pencil(dz_ref, zu)
-    arrived(yu, fy - 1, 4)
-    pencil(dy_ref, yu)
+    pencil(dz_ref, flat(zu))
     for i in range(3):
         acc[9 + i : 10 + i] = terms[i]
 
@@ -340,7 +340,7 @@
             y_block, y_block, vmem(fz, cz, nx),
             y_block, vmem(fz, cz, nx), y_block, vmem(fz, cz, nx),
             y_block, y_block, vmem(fz, cz, nx),
-            vmem(cy // 2, cz, nx), vmem(cy // 2, cz, half), vmem(cy, cz, half), vmem(columns, cy // 2 * cz, nx),
+            vmem(cy // 2, cz, nx), vmem(cy // 2, cz, half), vmem(cy, cz, half), vmem(cy, cz, columns * nx),
             vmem(16, 128), vmem(1, 128), vmem(1, 128), vmem(1, 128), vmem(fy * poles * fz // 2, 1, 128), vmem(8, 128),
             pltpu.SemaphoreType.DMA((8,)),
             pltpu.SemaphoreType.DMA((10,)),

time: 37.3 us -> 36.2 us (0.971)
  Pallas kernels: 35.4 us -> 34.2 us
    pallas_call x1, Pallas kernels: 35.4 us -> 34.2 us  [local(): pl.pallas_call(functools.partial(kernel, cy, cz, nx, fy, fz, poles), out_...]
where the time goes in v6:
time: 36.2 us; the launch traced here: 36.1 us
  Pallas kernels  34.2 us (94%)
  local copies, waits for them, and re-layouts  0.65 us (2%)
  between operations  0.64 us (2%)
  other arithmetic  0.57 us (2%)
    pallas_call x1, Pallas kernels, local(): pl.pallas_call(functools.partial(kernel, cy, cz, nx, fy, fz, poles), out_...  34.2 us

profile of v6, /device:TPU:1, one launch (start us, length us, event | category | flops | bytes accessed | tf_op | source)
XLA Modules:
  0.0 36.1 jit_solution(10861252047314763235)
XLA Ops:
  0.6 34.2 %shard_map.76 = (f32[1,16,8,256]{3,2,1,0:T(8,128)S(1)}, f32[2,2]{1,0:T(2,128)S(1)}, f32[2,2]{1,0:T(2,128)S(1)}) custom-call(f32[2,16,8,256]{3,2,1,0:T(8,128)} %states_hbm.1, f32[16,8,256]{2,1,0:T(8,128)} %pot_hbm.1, f32[256,256]{1,0:T(8,128)} %constant.6.clone.dx_hbm, f32[128,128]{1,0:T(8,128)} %constant.7.clone.dy_hbm.dz_hbm, ...), custom_call_target="tpu_custom_call" | custom-call | tf_op jit(solution)/shard_map/pallas_call | solution.py:327
  34.9 0.6 %broadcast_multiply_fusion = (f32[2,2]{1,0:T(2,128)}, f32[2,2]{1,0:T(2,128)}) fusion(f32[2,2]{1,0:T(2,128)S(1)} %get-tuple-element.8, f32[2,2]{1,0:T(2,128)S(1)} %get-tuple-element.7), kind=kLoop, calls=%fused_computation | loop fusion | flops 8 | bytes 64 | tf_op jit(solution)/shard_map/mul | solution.py:365
  35.4 0.7 %copy.9 = f32[1,16,8,256]{3,2,1,0:T(8,128)} copy(f32[1,16,8,256]{3,2,1,0:T(8,128)S(1)} %get-tuple-element.14) | data formatting | bytes 262144

commit v7 on v6

--- a/solution.py
+++ b/solution.py
@@ -37,8 +37,9 @@
     cy, cz, nx, fy, fz, poles,
     states_hbm, pot_hbm, dx_hbm, dy_hbm, dz_hbm,
     out_ref, corr_ref, energy_ref,
-    own_b, far_b, v_ref, dx_ref, dy_ref, dz_ref, s_ref, u_ref,
-    ysend, yb, zb, ymul, zmul, yback, zback, yusend, yu, zu, far_u, far_w, u_far, xmul,
+    own_b, far_b, v_ref, dx_ref, dy_ref, dz_ref, g_ref, s_ref, q_ref, u_ref, y_ref, dxs_ref, dxg_ref, far_u,
+    ysend, ysend2, yb, yq, ymul, ymul2, yback, yback2, z_order,
+    zb, zq, zmul, zmul2, zback, zback2,
     acc, mine_sums, core_sums, chip_sums, parts, rows_ref,
     load_sem, send_sem, recv_sem,
 ):
@@ -47,7 +48,6 @@
     plane = pole * fz + mz
     rows = cy * cz
     half = nx // 2
-    split = cy // 2
     col0, col1 = slice(0, half), slice(half, nx)
 
     def lane_block(index):
@@ -58,10 +58,6 @@
 
     def at_z(step):
         return (pole, my, lax.rem(mz + step, fz))
-
-    def at_plane(step):
-        other = lax.rem(plane + step, poles * fz)
-        return (other // fz, my, lax.rem(other, fz))
 
     def push(src, dst, place, slot):
         pltpu.make_async_remote_copy(
@@ -115,55 +111,89 @@
     rest = [
         load(states_hbm.at[c, :, :, lane_block(partner)], far_b.at[:, :, pl.ds(c * half, half)], 2 + c) for c in range(2)
     ]
-    rest.append(load(pot_hbm.at[:, :, lane_block(pole)], v_ref, 4))
-    rest.append(load(dx_hbm, dx_ref, 5))
-    rest.append(load(dz_hbm, dz_ref, 6))
-    rest.append(load(dy_hbm, dy_ref, 7))
+    rest.append(load(pot_hbm.at[:, :, lane_block(pole)], v_ref.at[:, :, pl.ds(0, half)], 4))
+    rest.append(load(pot_hbm.at[:, :, lane_block(partner)], v_ref.at[:, :, pl.ds(half, half)], 5))
+    rest.append(load(dx_hbm, dx_ref, 6))
+    rest.append(load(dz_hbm, dz_ref, 7))
+    rest.append(load(dy_hbm, dy_ref, 8))
     for copy in near:
         copy.wait()
     ysend[...] = jnp.swapaxes(own_b[...], 0, 1)
+    for copy in rest:
+        copy.wait()
+
+    def flat(ref):
+        return ref[...].reshape(rows, nx)
+
+    def column(ref, c):
+        return ref[:, :, c * half : (c + 1) * half].reshape(-1, half)
+
+    terms = [jnp.zeros((1, half), jnp.float32)] * 3
+
+    def quadratic(left, right):
+        terms[0] += lanes(left[0] * right[0])
+        terms[1] += lanes(left[0] * right[1])
+        terms[2] += lanes(left[1] * right[1])
+
+    def symmetric(left, right):
+        terms[0] += 2.0 * lanes(left[0] * right[0])
+        terms[1] += lanes(left[0] * right[1] + left[1] * right[0])
+        terms[2] += 2.0 * lanes(left[1] * right[1])
+
+    v = v_ref[...].reshape(rows, nx)
+    b = [column(own_b, c) for c in range(2)]
+    g, s = [], []
+    for c in range(2):
+        whole = jnp.concatenate([b[c], column(far_b, c)], axis=1)
+        g.append(dot(whole, dx_ref[...]))
+        s.append(v * whole + g[c])
+        here = slice(c * half, (c + 1) * half)
+        s_ref[:, :, here] = s[c][:, col0].reshape(cy, cz, half)
+        g_ref[:, :, here] = g[c][:, col0].reshape(cy, cz, half)
+        q_ref[:, :, here] = (s[c][:, col0] + 0.5 * g[c][:, col0]).reshape(cy, cz, half)
+    ysend2[...] = jnp.swapaxes(q_ref[...], 0, 1)
+
     pl.semaphore_wait(barrier, fy + fz - 1)
-
     scatter_y(ysend, yb, 0)
     scatter_z(own_b, zb, 1)
-    for copy in rest:
-        copy.wait()
-
-    def flat(ref):
-        return ref[...].reshape(rows, nx)
-
-    def column(ref, c):
-        return ref[:, :, c * half : (c + 1) * half].reshape(-1, half)
-
-    v = v_ref[...].reshape(rows, half)
-    b = [column(own_b, c) for c in range(2)]
-    s = []
-    for c in range(2):
-        whole = jnp.concatenate([b[c], column(far_b, c)], axis=1)
-        s.append(v * b[c] + dot(whole, dx_ref[:, col0]))
-        s_ref[:, :, c * half : (c + 1) * half] = s[c].reshape(cy, cz, half)
+    scatter_z(q_ref, zq, 3)
+    scatter_y(ysend2, yq, 2)
+
     acc[0:1] = lanes(b[0] * b[0])
     acc[1:2] = lanes(b[0] * b[1])
     acc[2:3] = lanes(b[1] * b[1])
     acc[12:16] = jnp.zeros((4, 128), jnp.float32)
+    for c in range(2):
+        here = slice(c * half, (c + 1) * half)
+        dxs_ref[:, :, here] = dot(s[c], dx_ref[:, col0]).reshape(cy, cz, half)
+        dxg_ref[:, :, here] = dot(g[c], dx_ref[:, col0]).reshape(cy, cz, half)
+    quadratic([s[c][:, col0] for c in range(2)], [column(dxs_ref, c) for c in range(2)])
 
     arrived(zb, fz - 1, 1)
     zmul[...] = dot(dz_ref[...], flat(zb)).reshape(fz, cz, nx)
-    scatter_z(zmul, zback, 3)
+    scatter_z(zmul, zback, 5)
     arrived(yb, fy - 1, 0)
     ymul[...] = dot(dy_ref[...], flat(yb)).reshape(fy, cy, nx)
-    scatter_y(ymul, yback, 2)
-
-    arrived(zback, fz - 1, 3)
-    s_ref[...] += zback[...]
-    yusend[...] = jnp.swapaxes(s_ref[...], 0, 1)
-    scatter_y(yusend, yu, 4)
-    arrived(yback, fy - 1, 2)
-    u_ref[...] = s_ref[...] + jnp.swapaxes(yback[...], 0, 1)
-    scatter_z(u_ref, zu, 5)
-    push(u_ref.at[pl.ds(partner * split, split)], far_u, across, 6)
-    push(u_ref.at[pl.ds(pole * split, split), :, lane_block(partner)], far_w, across, 7)
-
+    scatter_y(ymul, yback, 4)
+    ymul2[...] = dot(dy_ref[...], flat(ymul)).reshape(fy, cy, nx)
+    scatter_y(ymul2, yback2, 6)
+    z_twice = dot(dz_ref[...], flat(zmul))
+    arrived(zq, fz - 1, 3)
+    p = flat(zq) + flat(zmul)
+    p_mul = dot(dz_ref[...], p)
+    zmul2[...] = (4.0 * p_mul - z_twice).reshape(fz, cz, nx)
+    scatter_z(zmul2, zback2, 7)
+    quadratic([p[:, col0], p[:, col1]], [p_mul[:, col0], p_mul[:, col1]])
+    arrived(yq, fy - 1, 2)
+    p = flat(yq) + flat(ymul)
+    p_mul = dot(dy_ref[...], flat(yq)) + flat(ymul2)
+    quadratic([p[:, col0], p[:, col1]], [p_mul[:, col0], p_mul[:, col1]])
+
+    arrived(zback, fz - 1, 5)
+    arrived(yback, fy - 1, 4)
+    y_ref[...] = jnp.swapaxes(yback[...], 0, 1)
+    u_ref[...] = s_ref[...] + zback[...] + y_ref[...]
+    push(u_ref.at[:, :, lane_block(partner)], far_u, across, 10)
     u = [column(u_ref, c) for c in range(2)]
     acc[3:4] = lanes(b[0] * u[0])
     acc[4:5] = lanes(b[0] * u[1])
@@ -171,33 +201,16 @@
     acc[6:7] = lanes(u[0] * u[0])
     acc[7:8] = lanes(u[0] * u[1])
     acc[8:9] = lanes(u[1] * u[1])
-    applied = [v * u[0], v * u[1]]
-    terms = [lanes(u[0] * applied[0]), lanes(u[0] * applied[1]), lanes(u[1] * applied[1])]
-
-    def quadratic(left, right):
-        terms[0] += lanes(left[0] * right[0])
-        terms[1] += lanes(left[0] * right[1])
-        terms[2] += lanes(left[1] * right[1])
-
-    for c in range(2):
-        xmul[:, :, c * nx : (c + 1) * nx] = dot(u[c], dx_ref[0:half, :]).reshape(cy, cz, 2 * half)
-    quadratic(u, [xmul[:, :, c * nx : c * nx + half].reshape(rows, half) for c in range(2)])
-    mine, others = pl.ds(pole * split, split), pl.ds(partner * split, split)
-    between = [xmul[mine, :, c * nx + half : (c + 1) * nx].reshape(-1, half) for c in range(2)]
-
-    def pencil(operator, left):
-        product = dot(operator[...], left)
-        quadratic([left[:, col0], left[:, col1]], [product[:, col0], product[:, col1]])
-
-    arrived(yu, fy - 1, 4)
-    pencil(dy_ref, flat(yu) + flat(ymul))
-    arrived(far_u, split, 6)
-    far = [column(far_u, c) for c in range(2)]
-    terms[0] += 2.0 * lanes(far[0] * between[0])
-    terms[1] += lanes(far[0] * between[1] + far[1] * between[0])
-    terms[2] += 2.0 * lanes(far[1] * between[1])
-    arrived(zu, fz - 1, 5)
-    pencil(dz_ref, flat(zu))
+    quadratic(u, [v[:, col0] * u[c] for c in range(2)])
+    symmetric(
+        [0.5 * column(dxs_ref, c) - 0.125 * column(dxg_ref, c) for c in range(2)],
+        [column(y_ref, c) + column(zback, c) for c in range(2)],
+    )
+    z_order[...] = 1.5 * jnp.swapaxes(zback[...], 0, 1)
+    arrived(zback2, fz - 1, 7)
+    symmetric([0.5 * column(y_ref, c) for c in range(2)], [column(zback2, c) for c in range(2)])
+    arrived(yback2, fy - 1, 6)
+    symmetric([column(z_order, c) for c in range(2)], [column(yback2, c) for c in range(2)])
     for i in range(3):
         acc[9 + i : 10 + i] = terms[i]
 
@@ -210,10 +223,6 @@
     push(mine_sums, core_sums, (pole, my, mz + 1 - 2 * lax.rem(mz, 2)), 8)
 
     first = pole == 0
-    arrived(far_w, split, 7)
-    u_far[mine] = far_u[:, :, lane_block(pole)]
-    u_far[others] = far_w[...]
-
     whole_core = core_sums.at[pl.ds(0, 1)]
     pltpu.make_async_copy(whole_core, whole_core, recv_sem.at[8]).wait()
     chips = poles * fz // 2
@@ -230,14 +239,11 @@
         lax.fori_loop(0 if step_y else 1, chips, body, 0)
     parts[chip] = chip_sums[...]
 
-    sent(yb, fy - 1, 0)
-    sent(zb, fz - 1, 1)
-    sent(yback, fy - 1, 2)
-    sent(zback, fz - 1, 3)
-    sent(yu, fy - 1, 4)
-    sent(zu, fz - 1, 5)
-    sent(far_u, split, 6)
-    sent(far_w, split, 7)
+    for slot, (y_buffer, z_buffer) in zip((0, 2, 4, 6), ((yb, zb), (yq, zq), (yback, zback), (yback2, zback2))):
+        sent(y_buffer, fy - 1, slot)
+        sent(z_buffer, fz - 1, slot + 1)
+    arrived(far_u, cy, 10)
+    sent(far_u, cy, 10)
     pltpu.make_async_copy(whole_core, whole_core, send_sem.at[8]).wait()
 
     arrived(parts, fy * chips - 1, 9)
@@ -292,7 +298,7 @@
     column_block = lane_block(pole)
     for block, base, applied in (
         (lane_block(pole), own_b[:, :, column_block], u_ref[:, :, column_block]),
-        (lane_block(partner), far_b[:, :, column_block], u_far[...]),
+        (lane_block(partner), far_b[:, :, column_block], far_u[...]),
     ):
         out_ref[0, :, :, block] = a * base + f * (applied - my_mu * base)
     cross = a0 * a1 * m01 + a0 * f1 * c01 + f0 * a1 * c10 + f0 * f1 * w01
@@ -323,7 +329,7 @@
     def vmem(*shape):
         return pltpu.VMEM(shape, f32)
 
-    x_block, y_block = vmem(cy, cz, nx), vmem(fy, cy, nx)
+    x_block, y_block, z_block = vmem(cy, cz, nx), vmem(fy, cy, nx), vmem(fz, cz, nx)
     filtered, corr, energy = pl.pallas_call(
         functools.partial(kernel, cy, cz, nx, fy, fz, poles),
         out_shape=(
@@ -334,17 +340,15 @@
         in_specs=[in_hbm] * 5,
         out_specs=(in_vmem,) * 3,
         scratch_shapes=[
-            x_block, x_block, vmem(cy, cz, half),
+            *[x_block] * 3,
             vmem(nx, nx), vmem(cy * fy, cy * fy), vmem(cz * fz, cz * fz),
-            x_block, x_block,
-            y_block, y_block, vmem(fz, cz, nx),
-            y_block, vmem(fz, cz, nx), y_block, vmem(fz, cz, nx),
-            y_block, y_block, vmem(fz, cz, nx),
-            vmem(cy // 2, cz, nx), vmem(cy // 2, cz, half), vmem(cy, cz, half), vmem(cy, cz, columns * nx),
+            *[x_block] * 7, vmem(cy, cz, half),
+            *[y_block] * 9,
+            *[z_block] * 6,
             vmem(16, 128), vmem(1, 128), vmem(1, 128), vmem(1, 128), vmem(fy * poles * fz // 2, 1, 128), vmem(8, 128),
-            pltpu.SemaphoreType.DMA((8,)),
-            pltpu.SemaphoreType.DMA((10,)),
-            pltpu.SemaphoreType.DMA((10,)),
+            pltpu.SemaphoreType.DMA((9,)),
+            pltpu.SemaphoreType.DMA((11,)),
+            pltpu.SemaphoreType.DMA((11,)),
         ],
         compiler_params=pltpu.CompilerParams(
             collective_id=0, has_side_effects=True, vmem_limit_bytes=32 * 1024 * 1024

time: 36.2 us -> 34.9 us (0.964)
  Pallas kernels: 34.2 us -> 32.9 us
    pallas_call x1, Pallas kernels: 34.2 us -> 32.9 us  [local(): pl.pallas_call(functools.partial(kernel, cy, cz, nx, fy, fz, poles), out_...]
where the time goes in v7:
time: 34.9 us; the launch traced here: 34.7 us
  Pallas kernels  32.9 us (94%)
  local copies, waits for them, and re-layouts  0.65 us (2%)
  between operations  0.64 us (2%)
  other arithmetic  0.57 us (2%)
    pallas_call x1, Pallas kernels, local(): pl.pallas_call(functools.partial(kernel, cy, cz, nx, fy, fz, poles), out_...  32.9 us

profile of v7, /device:TPU:1, one launch (start us, length us, event | category | flops | bytes accessed | tf_op | source)
XLA Modules:
  0.0 34.7 jit_solution(5006449754786201029)
XLA Ops:
  0.6 32.9 %shard_map.76 = (f32[1,16,8,256]{3,2,1,0:T(8,128)S(1)}, f32[2,2]{1,0:T(2,128)S(1)}, f32[2,2]{1,0:T(2,128)S(1)}) custom-call(f32[2,16,8,256]{3,2,1,0:T(8,128)} %states_hbm.1, f32[16,8,256]{2,1,0:T(8,128)} %pot_hbm.1, f32[256,256]{1,0:T(8,128)} %constant.6.clone.dx_hbm, f32[128,128]{1,0:T(8,128)} %constant.7.clone.dy_hbm.dz_hbm, ...), custom_call_target="tpu_custom_call" | custom-call | tf_op jit(solution)/shard_map/pallas_call | solution.py:333
  33.5 0.6 %broadcast_multiply_fusion = (f32[2,2]{1,0:T(2,128)}, f32[2,2]{1,0:T(2,128)}) fusion(f32[2,2]{1,0:T(2,128)S(1)} %get-tuple-element.8, f32[2,2]{1,0:T(2,128)S(1)} %get-tuple-element.7), kind=kLoop, calls=%fused_computation | loop fusion | flops 8 | bytes 64 | tf_op jit(solution)/shard_map/mul | solution.py:369
  34.1 0.7 %copy.9 = f32[1,16,8,256]{3,2,1,0:T(8,128)} copy(f32[1,16,8,256]{3,2,1,0:T(8,128)S(1)} %get-tuple-element.14) | data formatting | bytes 262144

commit v8 on v7

--- a/solution.py
+++ b/solution.py
@@ -45,7 +45,6 @@
 ):
     pole, my, mz = lax.axis_index("pole"), lax.axis_index("fy"), lax.axis_index("fz")
     partner = 1 - pole
-    plane = pole * fz + mz
     rows = cy * cz
     half = nx // 2
     col0, col1 = slice(0, half), slice(half, nx)
@@ -93,6 +92,7 @@
         whole = dst.at[pl.ds(0, count)]
         pltpu.make_async_copy(whole, whole, send_sem.at[slot]).wait()
 
+    parts[...] = jnp.zeros(parts.shape, jnp.float32)
     barrier = pltpu.get_barrier_semaphore()
 
     for step in far_first(fy):
@@ -220,24 +220,44 @@
     for shift in (64, 32, 16, 8):
         folded = folded + pltpu.roll(folded, shift, 1)
     mine_sums[...] = jnp.sum(jnp.where(lane // 8 == row, folded, 0.0), axis=0, keepdims=True)
-    push(mine_sums, core_sums, (pole, my, mz + 1 - 2 * lax.rem(mz, 2)), 8)
-
-    first = pole == 0
+
+    core = lax.rem(mz, 2)
+    push(mine_sums, core_sums, (pole, my, mz + 1 - 2 * core), 8)
+    size_x, size_y = 2 * poles, fz // 4
+    place_x = [lax.rem(2 * pole + lax.rem(mz // 2, 2) + k, size_x) for k in range(size_x)]
+    place_y = [lax.rem(mz // 4 + k, size_y) for k in range(size_y)]
+    place_z = [lax.rem(my + k, fy) for k in range(fy)]
+    pole_of = [x // 2 for x in place_x]
+    low_of = [2 * lax.rem(x, 2) for x in place_x]
+    chip = (my * size_y + mz // 4) * size_x + place_x[0]
+
+    def hops(offset):
+        return sum(min(k, n - k) for k, n in zip(offset, (size_x, size_y, fy)))
+
+    offsets = sorted(
+        ((x, y, z) for x in range(size_x) for y in range(size_y) for z in range(fy) if (x, y, z) != (0, 0, 0)),
+        key=lambda offset: -hops(offset),
+    )
+    far_away = [offset for offset in offsets if hops(offset) >= hops(offsets[0]) - 2]
+
+    def device(offset, which):
+        x, y, z = offset
+        return (pole_of[x], place_z[z], place_y[y] * 4 + low_of[x] + which)
+
+    chips = size_x * size_y * fy
+    mine_row = pl.ds(core * chips + chip, 1)
+    pair_row = pl.ds(chip, 1)
+    for offset in far_away:
+        for which in range(2):
+            push(mine_sums, parts.at[mine_row], device(offset, which), 9)
+
     whole_core = core_sums.at[pl.ds(0, 1)]
     pltpu.make_async_copy(whole_core, whole_core, recv_sem.at[8]).wait()
-    chips = poles * fz // 2
-    chip = my * chips + plane // 2
     chip_sums[...] = mine_sums[...] + core_sums[...]
-    for step_y in far_first(fy) + [0]:
-
-        def body(step, carry, step_y=step_y):
-            other = lax.rem(plane + 2 * step, 2 * chips)
-            place = (other // fz, lax.rem(my + step_y, fy), lax.rem(other, fz))
-            push(chip_sums, parts.at[chip], place, 9)
-            return carry
-
-        lax.fori_loop(0 if step_y else 1, chips, body, 0)
-    parts[chip] = chip_sums[...]
+    for offset in offsets[len(far_away) :]:
+        push(chip_sums, parts.at[pair_row], device(offset, core), 9)
+    parts[pair_row, :] = chip_sums[...]
+    messages = len(offsets) + len(far_away)
 
     for slot, (y_buffer, z_buffer) in zip((0, 2, 4, 6), ((yb, zb), (yq, zq), (yback, zback), (yback2, zback2))):
         sent(y_buffer, fy - 1, slot)
@@ -246,8 +266,8 @@
     sent(far_u, cy, 10)
     pltpu.make_async_copy(whole_core, whole_core, send_sem.at[8]).wait()
 
-    arrived(parts, fy * chips - 1, 9)
-    total = jnp.sum(parts[...], axis=0)
+    arrived(parts, messages, 9)
+    total = jnp.sum(parts[0:chips] + parts[chips : 2 * chips], axis=0, keepdims=True)
     slim = lax.broadcasted_iota(jnp.int32, (8, 128), 1) < 8
 
     def totals(values):
@@ -293,6 +313,7 @@
 
     a0, f0 = factors(mu[0], m00, w00, e00)
     a1, f1 = factors(mu[1], m11, w11, e11)
+    first = pole == 0
     a, f = jnp.where(first, a0, a1), jnp.where(first, f0, f1)
     my_mu = jnp.where(first, mu[0], mu[1])
     column_block = lane_block(pole)
@@ -315,7 +336,7 @@
         cross,
         a1 * a1 * mu[1] * m11 + 2.0 * a1 * f1 * w11 + f1 * f1 * e11,
     )
-    sent(parts, fy * chips - 1, 9)
+    sent(parts, messages, 9)
 
 
 def local(states, potential):
@@ -345,7 +366,7 @@
             *[x_block] * 7, vmem(cy, cz, half),
             *[y_block] * 9,
             *[z_block] * 6,
-            vmem(16, 128), vmem(1, 128), vmem(1, 128), vmem(1, 128), vmem(fy * poles * fz // 2, 1, 128), vmem(8, 128),
+            vmem(16, 128), vmem(1, 128), vmem(1, 128), vmem(1, 128), vmem(fy * poles * fz, 128), vmem(8, 128),
             pltpu.SemaphoreType.DMA((9,)),
             pltpu.SemaphoreType.DMA((11,)),
             pltpu.SemaphoreType.DMA((11,)),

time: 34.9 us -> 34.2 us (0.980)
  Pallas kernels: 32.9 us -> 32.2 us
    pallas_call x1, Pallas kernels: 32.9 us -> 32.2 us  [local(): pl.pallas_call(functools.partial(kernel, cy, cz, nx, fy, fz, poles), out_...]
where the time goes in v8:
time: 34.2 us; the launch traced here: 34.1 us
  Pallas kernels  32.2 us (94%)
  local copies, waits for them, and re-layouts  0.65 us (2%)
  between operations  0.64 us (2%)
  other arithmetic  0.57 us (2%)
    pallas_call x1, Pallas kernels, local(): pl.pallas_call(functools.partial(kernel, cy, cz, nx, fy, fz, poles), out_...  32.2 us

profile of v8, /device:TPU:1, one launch (start us, length us, event | category | flops | bytes accessed | tf_op | source)
XLA Modules:
  0.0 34.1 jit_solution(9561803777659415960)
XLA Ops:
  0.6 32.2 %shard_map.76 = (f32[1,16,8,256]{3,2,1,0:T(8,128)S(1)}, f32[2,2]{1,0:T(2,128)S(1)}, f32[2,2]{1,0:T(2,128)S(1)}) custom-call(f32[2,16,8,256]{3,2,1,0:T(8,128)} %states_hbm.1, f32[16,8,256]{2,1,0:T(8,128)} %pot_hbm.1, f32[256,256]{1,0:T(8,128)} %constant.6.clone.dx_hbm, f32[128,128]{1,0:T(8,128)} %constant.7.clone.dy_hbm.dz_hbm, ...), custom_call_target="tpu_custom_call" | custom-call | tf_op jit(solution)/shard_map/pallas_call | solution.py:354
  32.8 0.6 %broadcast_multiply_fusion = (f32[2,2]{1,0:T(2,128)}, f32[2,2]{1,0:T(2,128)}) fusion(f32[2,2]{1,0:T(2,128)S(1)} %get-tuple-element.8, f32[2,2]{1,0:T(2,128)S(1)} %get-tuple-element.7), kind=kLoop, calls=%fused_computation | loop fusion | flops 8 | bytes 64 | tf_op jit(solution)/shard_map/mul | solution.py:390
  33.4 0.7 %copy.9 = f32[1,16,8,256]{3,2,1,0:T(8,128)} copy(f32[1,16,8,256]{3,2,1,0:T(8,128)S(1)} %get-tuple-element.14) | data formatting | bytes 262144

commit v9 on v8

--- a/solution.py
+++ b/solution.py
@@ -38,7 +38,7 @@
     states_hbm, pot_hbm, dx_hbm, dy_hbm, dz_hbm,
     out_ref, corr_ref, energy_ref,
     own_b, far_b, v_ref, dx_ref, dy_ref, dz_ref, g_ref, s_ref, q_ref, u_ref, y_ref, dxs_ref, dxg_ref, far_u,
-    ysend, ysend2, yb, yq, ymul, ymul2, yback, yback2, z_order,
+    ysend, yb, ymul, ymul2, yback, yback2, vsend, yv, z_order, g_order,
     zb, zq, zmul, zmul2, zback, zback2,
     acc, mine_sums, core_sums, chip_sums, parts, rows_ref,
     load_sem, send_sem, recv_sem,
@@ -118,7 +118,8 @@
     rest.append(load(dy_hbm, dy_ref, 8))
     for copy in near:
         copy.wait()
-    ysend[...] = jnp.swapaxes(own_b[...], 0, 1)
+    for c in range(2):
+        ysend[c] = jnp.swapaxes(own_b[:, :, c * half : (c + 1) * half], 0, 1)
     for copy in rest:
         copy.wait()
 
@@ -151,13 +152,15 @@
         s_ref[:, :, here] = s[c][:, col0].reshape(cy, cz, half)
         g_ref[:, :, here] = g[c][:, col0].reshape(cy, cz, half)
         q_ref[:, :, here] = (s[c][:, col0] + 0.5 * g[c][:, col0]).reshape(cy, cz, half)
-    ysend2[...] = jnp.swapaxes(q_ref[...], 0, 1)
+    vsend[...] = jnp.swapaxes(v_ref[:, :, 0:half], 0, 1)
+    g_order[...] = jnp.swapaxes(g_ref[...], 0, 1)
 
     pl.semaphore_wait(barrier, fy + fz - 1)
-    scatter_y(ysend, yb, 0)
+    scatter_y(ysend.at[0], yb.at[0], 0)
+    scatter_y(ysend.at[1], yb.at[1], 11)
     scatter_z(own_b, zb, 1)
+    scatter_y(vsend, yv, 2)
     scatter_z(q_ref, zq, 3)
-    scatter_y(ysend2, yq, 2)
 
     acc[0:1] = lanes(b[0] * b[0])
     acc[1:2] = lanes(b[0] * b[1])
@@ -169,14 +172,22 @@
         dxg_ref[:, :, here] = dot(g[c], dx_ref[:, col0]).reshape(cy, cz, half)
     quadratic([s[c][:, col0] for c in range(2)], [column(dxs_ref, c) for c in range(2)])
 
+    def y_column(c, slot, slot2):
+        ymul[c] = dot(dy_ref[...], yb[c].reshape(-1, half)).reshape(fy, cy, half)
+        ymul2[c] = dot(dy_ref[...], ymul[c].reshape(-1, half)).reshape(fy, cy, half)
+        for step in far_first(fy):
+            push_y(ymul.at[c], yback.at[c], step, slot)
+            push_y(ymul2.at[c], yback2.at[c], step, slot2)
+        yback[c, my] = ymul[c, my]
+        yback2[c, my] = ymul2[c, my]
+
+    arrived(yb.at[0], fy - 1, 0)
+    y_column(0, 4, 6)
+    arrived(yb.at[1], fy - 1, 11)
+    y_column(1, 12, 13)
     arrived(zb, fz - 1, 1)
     zmul[...] = dot(dz_ref[...], flat(zb)).reshape(fz, cz, nx)
     scatter_z(zmul, zback, 5)
-    arrived(yb, fy - 1, 0)
-    ymul[...] = dot(dy_ref[...], flat(yb)).reshape(fy, cy, nx)
-    scatter_y(ymul, yback, 4)
-    ymul2[...] = dot(dy_ref[...], flat(ymul)).reshape(fy, cy, nx)
-    scatter_y(ymul2, yback2, 6)
     z_twice = dot(dz_ref[...], flat(zmul))
     arrived(zq, fz - 1, 3)
     p = flat(zq) + flat(zmul)
@@ -184,14 +195,15 @@
     zmul2[...] = (4.0 * p_mul - z_twice).reshape(fz, cz, nx)
     scatter_z(zmul2, zback2, 7)
     quadratic([p[:, col0], p[:, col1]], [p_mul[:, col0], p_mul[:, col1]])
-    arrived(yq, fy - 1, 2)
-    p = flat(yq) + flat(ymul)
-    p_mul = dot(dy_ref[...], flat(yq)) + flat(ymul2)
-    quadratic([p[:, col0], p[:, col1]], [p_mul[:, col0], p_mul[:, col1]])
+    arrived(yv, fy - 1, 2)
+    h = [(yv[...] * yb[c]).reshape(-1, half) for c in range(2)]
+    p_mul = [dot(dy_ref[...], h[c]) + ymul2[c].reshape(-1, half) for c in range(2)]
+    quadratic([h[c] + ymul[c].reshape(-1, half) for c in range(2)], p_mul)
 
     arrived(zback, fz - 1, 5)
-    arrived(yback, fy - 1, 4)
-    y_ref[...] = jnp.swapaxes(yback[...], 0, 1)
+    for c, slot in ((0, 4), (1, 12)):
+        arrived(yback.at[c], fy - 1, slot)
+        y_ref[:, :, c * half : (c + 1) * half] = jnp.swapaxes(yback[c], 0, 1)
     u_ref[...] = s_ref[...] + zback[...] + y_ref[...]
     push(u_ref.at[:, :, lane_block(partner)], far_u, across, 10)
     u = [column(u_ref, c) for c in range(2)]
@@ -202,15 +214,18 @@
     acc[7:8] = lanes(u[0] * u[1])
     acc[8:9] = lanes(u[1] * u[1])
     quadratic(u, [v[:, col0] * u[c] for c in range(2)])
+    y = [column(y_ref, c) for c in range(2)]
+    symmetric([2.0 * column(dxs_ref, c) - 0.5 * column(dxg_ref, c) for c in range(2)], y)
     symmetric(
         [0.5 * column(dxs_ref, c) - 0.125 * column(dxg_ref, c) for c in range(2)],
-        [column(y_ref, c) + column(zback, c) for c in range(2)],
-    )
-    z_order[...] = 1.5 * jnp.swapaxes(zback[...], 0, 1)
+        [column(zback, c) for c in range(2)],
+    )
+    z_order[...] = 1.5 * (g_order[...] + jnp.swapaxes(zback[...], 0, 1))
     arrived(zback2, fz - 1, 7)
-    symmetric([0.5 * column(y_ref, c) for c in range(2)], [column(zback2, c) for c in range(2)])
-    arrived(yback2, fy - 1, 6)
-    symmetric([column(z_order, c) for c in range(2)], [column(yback2, c) for c in range(2)])
+    symmetric([0.5 * y[c] for c in range(2)], [column(zback2, c) for c in range(2)])
+    for c, slot in ((0, 6), (1, 13)):
+        arrived(yback2.at[c], fy - 1, slot)
+    symmetric([column(z_order, c) for c in range(2)], [yback2[c].reshape(-1, half) for c in range(2)])
     for i in range(3):
         acc[9 + i : 10 + i] = terms[i]
 
@@ -238,7 +253,7 @@
         ((x, y, z) for x in range(size_x) for y in range(size_y) for z in range(fy) if (x, y, z) != (0, 0, 0)),
         key=lambda offset: -hops(offset),
     )
-    far_away = [offset for offset in offsets if hops(offset) >= hops(offsets[0]) - 2]
+    far_away = [offset for offset in offsets if hops(offset) >= hops(offsets[0]) - 3]
 
     def device(offset, which):
         x, y, z = offset
@@ -259,9 +274,12 @@
     parts[pair_row, :] = chip_sums[...]
     messages = len(offsets) + len(far_away)
 
-    for slot, (y_buffer, z_buffer) in zip((0, 2, 4, 6), ((yb, zb), (yq, zq), (yback, zback), (yback2, zback2))):
-        sent(y_buffer, fy - 1, slot)
-        sent(z_buffer, fz - 1, slot + 1)
+    for slot, z_buffer in ((1, zb), (3, zq), (5, zback), (7, zback2)):
+        sent(z_buffer, fz - 1, slot)
+    for y_buffer, slots in ((yb, (0, 11)), (yback, (4, 12)), (yback2, (6, 13))):
+        for c in range(2):
+            sent(y_buffer.at[c], fy - 1, slots[c])
+    sent(yv, fy - 1, 2)
     arrived(far_u, cy, 10)
     sent(far_u, cy, 10)
     pltpu.make_async_copy(whole_core, whole_core, send_sem.at[8]).wait()
@@ -364,12 +382,12 @@
             *[x_block] * 3,
             vmem(nx, nx), vmem(cy * fy, cy * fy), vmem(cz * fz, cz * fz),
             *[x_block] * 7, vmem(cy, cz, half),
-            *[y_block] * 9,
+            *[vmem(columns, fy, cy, half)] * 6, vmem(fy, cy, half), vmem(fy, cy, half), y_block, y_block,
             *[z_block] * 6,
             vmem(16, 128), vmem(1, 128), vmem(1, 128), vmem(1, 128), vmem(fy * poles * fz, 128), vmem(8, 128),
             pltpu.SemaphoreType.DMA((9,)),
-            pltpu.SemaphoreType.DMA((11,)),
-            pltpu.SemaphoreType.DMA((11,)),
+            pltpu.SemaphoreType.DMA((14,)),
+            pltpu.SemaphoreType.DMA((14,)),
         ],
         compiler_params=pltpu.CompilerParams(
             collective_id=0, has_side_effects=True, vmem_limit_bytes=32 * 1024 * 1024

time: 34.2 us -> 32.8 us (0.959)
  Pallas kernels: 32.2 us -> 30.9 us
    pallas_call x1, Pallas kernels: 32.2 us -> 30.9 us  [local(): pl.pallas_call(functools.partial(kernel, cy, cz, nx, fy, fz, poles), out_...]
where the time goes in v9:
time: 32.8 us; the launch traced here: 32.7 us
  Pallas kernels  30.9 us (94%)
  local copies, waits for them, and re-layouts  0.65 us (2%)
  between operations  0.64 us (2%)
  other arithmetic  0.57 us (2%)
    pallas_call x1, Pallas kernels, local(): pl.pallas_call(functools.partial(kernel, cy, cz, nx, fy, fz, poles), out_...  30.9 us

profile of v9, /device:TPU:1, one launch (start us, length us, event | category | flops | bytes accessed | tf_op | source)
XLA Modules:
  0.0 32.7 jit_solution(5026337894078985089)
XLA Ops:
  0.6 30.9 %shard_map.76 = (f32[1,16,8,256]{3,2,1,0:T(8,128)S(1)}, f32[2,2]{1,0:T(2,128)S(1)}, f32[2,2]{1,0:T(2,128)S(1)}) custom-call(f32[2,16,8,256]{3,2,1,0:T(8,128)} %states_hbm.1, f32[16,8,256]{2,1,0:T(8,128)} %pot_hbm.1, f32[256,256]{1,0:T(8,128)} %constant.6.clone.dx_hbm, f32[128,128]{1,0:T(8,128)} %constant.7.clone.dy_hbm.dz_hbm, ...), custom_call_target="tpu_custom_call" | custom-call | tf_op jit(solution)/shard_map/pallas_call | solution.py:372
  31.5 0.6 %broadcast_multiply_fusion = (f32[2,2]{1,0:T(2,128)}, f32[2,2]{1,0:T(2,128)}) fusion(f32[2,2]{1,0:T(2,128)S(1)} %get-tuple-element.8, f32[2,2]{1,0:T(2,128)S(1)} %get-tuple-element.7), kind=kLoop, calls=%fused_computation | loop fusion | flops 8 | bytes 64 | tf_op jit(solution)/shard_map/mul | solution.py:408
  32.1 0.7 %copy.9 = f32[1,16,8,256]{3,2,1,0:T(8,128)} copy(f32[1,16,8,256]{3,2,1,0:T(8,128)S(1)} %get-tuple-element.14) | data formatting | bytes 262144

commit v10 on v9

--- a/solution.py
+++ b/solution.py
@@ -324,10 +324,12 @@
         size = real * real + imag * imag
         return ((det - q * trace) * imag - real) / size, trace * imag / size
 
+    per_cell = 1.0 / float(nx * cy * fy * cz * fz)
+
     def gram(ref, upper, cross, lower):
         lane = lax.broadcasted_iota(jnp.int32, (1, 128), 1)
-        ref[0:1, :] = jnp.where(lane == 0, upper, cross)[:, 0:2]
-        ref[1:2, :] = jnp.where(lane == 0, cross, lower)[:, 0:2]
+        ref[0:1, :] = (jnp.where(lane == 0, upper, cross) * per_cell)[:, 0:2]
+        ref[1:2, :] = (jnp.where(lane == 0, cross, lower) * per_cell)[:, 0:2]
 
     a0, f0 = factors(mu[0], m00, w00, e00)
     a1, f1 = factors(mu[1], m11, w11, e11)
@@ -404,8 +406,23 @@
             )
         )
     )
-    cells = 1.0 / float(nx * cy * fy * cz * fz)
-    return filtered, corr * cells, energy * cells
+    outs = (filtered, corr, energy)
+    return pl.pallas_call(
+        store,
+        out_shape=tuple(jax.ShapeDtypeStruct(out.shape, f32) for out in outs),
+        in_specs=[in_vmem] * 3,
+        out_specs=(in_hbm,) * 3,
+        scratch_shapes=[pltpu.SemaphoreType.DMA((3,))],
+    )(*(pltpu.with_memory_space_constraint(out, pltpu.VMEM) for out in outs))
+
+
+def store(filtered, corr, energy, filtered_out, corr_out, energy_out, sem):
+    pairs = ((filtered, filtered_out), (corr, corr_out), (energy, energy_out))
+    copies = [pltpu.make_async_copy(src, dst, sem.at[i]) for i, (src, dst) in enumerate(pairs)]
+    for copy in copies:
+        copy.start()
+    for copy in copies:
+        copy.wait()
 
 
 def solution(mesh):

time: 32.8 us -> 32.3 us (0.985)
  Pallas kernels: 30.9 us -> 31.6 us
  local copies, waits for them, and re-layouts: 0.65 us -> 0 us
  other arithmetic: 0.57 us -> 0 us
    pallas_call x0 -> x1, Pallas kernels: none -> 0.69 us  [local(): pl.pallas_call(store, out_shape=tuple((jax.ShapeDtypeStruct(out.shape, f3...]
    unnamed x1 -> x0, local copies, waits for them, and re-layouts: 0.65 us -> none
    mul x1 -> x0, other arithmetic: 0.57 us -> none  [local(): return (filtered, corr * cells, energy * cells)]
where the time goes in v10:
time: 32.3 us; the launch traced here: 32.2 us
  Pallas kernels  31.6 us (98%)
  between operations  0.64 us (2%)
    pallas_call x1, Pallas kernels, local(): pl.pallas_call(functools.partial(kernel, cy, cz, nx, fy, fz, poles), out_...  30.9 us
    pallas_call x1, Pallas kernels, local(): pl.pallas_call(store, out_shape=tuple((jax.ShapeDtypeStruct(out.shape, f3...  0.69 us

profile of v10, /device:TPU:1, one launch (start us, length us, event | category | flops | bytes accessed | tf_op | source)
XLA Modules:
  0.0 32.2 jit_solution(3675204736698219116)
XLA Ops:
  0.6 30.9 %shard_map.76 = (f32[1,16,8,256]{3,2,1,0:T(8,128)S(1)}, f32[2,2]{1,0:T(2,128)S(1)}, f32[2,2]{1,0:T(2,128)S(1)}) custom-call(f32[2,16,8,256]{3,2,1,0:T(8,128)} %states_hbm.1, f32[16,8,256]{2,1,0:T(8,128)} %pot_hbm.1, f32[256,256]{1,0:T(8,128)} %constant.4.clone.dx_hbm, f32[128,128]{1,0:T(8,128)} %constant.5.clone.dy_hbm.dz_hbm, ...), custom_call_target="tpu_custom_call" | custom-call | tf_op jit(solution)/shard_map/pallas_call | solution.py:374
  31.5 0.7 %shard_map.77 = (f32[1,16,8,256]{3,2,1,0:T(8,128)}, f32[2,2]{1,0:T(2,128)}, f32[2,2]{1,0:T(2,128)}) custom-call(f32[1,16,8,256]{3,2,1,0:T(8,128)S(1)} %get-tuple-element.6.filtered, f32[2,2]{1,0:T(2,128)S(1)} %get-tuple-element.7.corr, f32[2,2]{1,0:T(2,128)S(1)} %get-tuple-element.8.energy), custom_call_target="tpu_custom_call" | custom-call | tf_op jit(solution)/shard_map/pallas_call | solution.py:410

commit v11 on v10

--- a/solution.py
+++ b/solution.py
@@ -223,17 +223,23 @@
     z_order[...] = 1.5 * (g_order[...] + jnp.swapaxes(zback[...], 0, 1))
     arrived(zback2, fz - 1, 7)
     symmetric([0.5 * y[c] for c in range(2)], [column(zback2, c) for c in range(2)])
-    for c, slot in ((0, 6), (1, 13)):
-        arrived(yback2.at[c], fy - 1, slot)
-    symmetric([column(z_order, c) for c in range(2)], [yback2[c].reshape(-1, half) for c in range(2)])
+    left = [column(z_order, c) for c in range(2)]
+    arrived(yback2.at[0], fy - 1, 6)
+    right = yback2[0].reshape(-1, half)
+    terms[0] += 2.0 * lanes(left[0] * right)
+    terms[1] += lanes(left[1] * right)
+    arrived(yback2.at[1], fy - 1, 13)
+    right = yback2[1].reshape(-1, half)
+    terms[1] += lanes(left[0] * right)
+    terms[2] += 2.0 * lanes(left[1] * right)
     for i in range(3):
         acc[9 + i : 10 + i] = terms[i]
 
     lane = lax.broadcasted_iota(jnp.int32, (16, 128), 1)
     row = lax.broadcasted_iota(jnp.int32, (16, 128), 0)
     folded = acc[...]
-    for shift in (64, 32, 16, 8):
-        folded = folded + pltpu.roll(folded, shift, 1)
+    for shifts in ((32, 64, 96), (8, 16, 24)):
+        folded = folded + sum(pltpu.roll(folded, shift, 1) for shift in shifts)
     mine_sums[...] = jnp.sum(jnp.where(lane // 8 == row, folded, 0.0), axis=0, keepdims=True)
 
     core = lax.rem(mz, 2)

time: 32.3 us -> 32.1 us (level)
  no operation moved by 1% of the time
where the time goes in v11:
time: 32.1 us; the launch traced here: 32 us
  Pallas kernels  31.4 us (98%)
  between operations  0.64 us (2%)
    pallas_call x1, Pallas kernels, local(): pl.pallas_call(functools.partial(kernel, cy, cz, nx, fy, fz, poles), out_...  30.7 us
    pallas_call x1, Pallas kernels, local(): pl.pallas_call(store, out_shape=tuple((jax.ShapeDtypeStruct(out.shape, f3...  0.69 us

profile of v11, /device:TPU:1, one launch (start us, length us, event | category | flops | bytes accessed | tf_op | source)
XLA Modules:
  0.0 32.0 jit_solution(3171029342097783690)
XLA Ops:
  0.6 30.7 %shard_map.76 = (f32[1,16,8,256]{3,2,1,0:T(8,128)S(1)}, f32[2,2]{1,0:T(2,128)S(1)}, f32[2,2]{1,0:T(2,128)S(1)}) custom-call(f32[2,16,8,256]{3,2,1,0:T(8,128)} %states_hbm.1, f32[16,8,256]{2,1,0:T(8,128)} %pot_hbm.1, f32[256,256]{1,0:T(8,128)} %constant.4.clone.dx_hbm, f32[128,128]{1,0:T(8,128)} %constant.5.clone.dy_hbm.dz_hbm, ...), custom_call_target="tpu_custom_call" | custom-call | tf_op jit(solution)/shard_map/pallas_call | solution.py:380
  31.4 0.7 %shard_map.77 = (f32[1,16,8,256]{3,2,1,0:T(8,128)}, f32[2,2]{1,0:T(2,128)}, f32[2,2]{1,0:T(2,128)}) custom-call(f32[1,16,8,256]{3,2,1,0:T(8,128)S(1)} %get-tuple-element.6.filtered, f32[2,2]{1,0:T(2,128)S(1)} %get-tuple-element.7.corr, f32[2,2]{1,0:T(2,128)S(1)} %get-tuple-element.8.energy), custom_call_target="tpu_custom_call" | custom-call | tf_op jit(solution)/shard_map/pallas_call | solution.py:416
